TPU v7x, 32 devices: a whole 2x2x4 slice. The times are simulated.
32 devices in a mesh: dp: 16 (over z, x, core), side: 2 (over y).
Axes of the slice: x: 2, y: 2, z: 4, core: 2. Of those that a mesh axis runs over, the one named last changes fastest.
Arguments:
- backbone_in: bfloat16 [65536, 768], P(('dp', 'side')), may hold values from -6 to 6
- segment_ids: int32 [65536], P('dp'), may hold values from 0 to 511, never falling along the last dimension, each value on 1 to 1024 neighbouring positions
- gate_index: int32 [1], replicated, may hold values from 0 to 11
- norm_before: float32 [768], replicated, may hold values from 0.5 to 1.5
- norm_middle: float32 [768], replicated, may hold values from 0.5 to 1.5
- frozen_query: bfloat16 [768, 768], replicated, may hold values from -0.21875 to 0.21875
- frozen_key: bfloat16 [768, 768], replicated, may hold values from -0.21875 to 0.21875
- frozen_value: bfloat16 [768, 768], replicated, may hold values from -0.21875 to 0.21875
- frozen_output: bfloat16 [768, 768], replicated, may hold values from -0.875 to 0.875
- frozen_expand: bfloat16 [768, 3072], replicated, may hold values from -0.21875 to 0.21875
- frozen_reduce: bfloat16 [3072, 768], replicated, may hold values from -0.109375 to 0.109375
- tap_weight: bfloat16 [768, 96], replicated, may hold values from -0.21875 to 0.21875
- gate_table: float32 [12, 96], replicated, may hold values from -6 to 6
- side_stream: bfloat16 [65536, 96], P(('dp', 'side')), may hold values from -6 to 6
- ladder_before: float32 [96], replicated, may hold values from 0.5 to 1.5
- ladder_middle: float32 [96], replicated, may hold values from 0.5 to 1.5
- ladder_query: bfloat16 [96, 96], P(None, 'side'), may hold values from -0.625 to 0.625
- ladder_key: bfloat16 [96, 96], P(None, 'side'), may hold values from -0.625 to 0.625
- ladder_value: bfloat16 [96, 96], P(None, 'side'), may hold values from -0.625 to 0.625
- ladder_output: bfloat16 [96, 96], P('side'), may hold values from -2.5 to 2.5
- ladder_expand: bfloat16 [96, 384], P(None, 'side'), may hold values from -0.625 to 0.625
- ladder_reduce: bfloat16 [384, 96], P('side'), may hold values from -0.4375 to 0.4375
- cotangent: bfloat16 [65536, 96], P(('dp', 'side')), may hold values from -6 to 6
Outputs:
- ladder_out: bfloat16 [65536, 96], P(('dp', 'side'))
- stream_grad: bfloat16 [65536, 96], P(('dp', 'side'))
- tap_grad: float32 [768, 96], replicated
- gate_grad: float32 [12, 96], replicated
- before_grad: float32 [96], replicated
- middle_grad: float32 [96], replicated
- query_grad: float32 [96, 96], P(None, 'side')
- key_grad: float32 [96, 96], P(None, 'side')
- value_grad: float32 [96, 96], P(None, 'side')
- output_grad: float32 [96, 96], P('side')
- expand_grad: float32 [96, 384], P(None, 'side')
- reduce_grad: float32 [384, 96], P('side')
Inputs may be any that keep to these rules, and one draw needn't show every extreme that they name: `segment_ids`: segment numbers never fall along the tokens; attention stays within one segment and one block of 1024 tokens.
All inputs are finite; a program needn't handle non-finite values.
Results may differ from a plain program's by a relative error of at most 0.033.
Values may be sent and summed in bfloat16 or wider, within the bound.
No kernel may reach another device: no remote copies, remote signals or barrier semaphores. Data moves between devices by JAX's collectives and lax.ppermute only.
A program may use at most 192 MiB of HBM per device.

v0:
```python
import functools

import jax
import jax.numpy as jnp
from jax import lax
from jax.experimental import pallas as pl
from jax.experimental.pallas import tpu as pltpu
from jax.sharding import PartitionSpec as P

HEAD = 64
SIDE_HEAD = 8
SEQ = 1024
EPS = 1e-06
MASKED = -1e30
LOG2E = 1.4426950408889634
SAFE = 64.0
TILE = 512
ROWS = 96
GROUP = 4
PAIRS = 2

F32 = jnp.float32
BF16 = jnp.bfloat16
NN = (((1,), (0,)), ((), ()))
NT = (((1,), (1,)), ((), ()))
TN = (((0,), (0,)), ((), ()))


def dot(left, right, dims=NN):
    return lax.dot_general(left, right, dims, preferred_element_type=F32)


def gelu_inner(values):
    return 0.7978845608028654 * values * (1.0 + 0.044715 * values * values)


def gelu(values):
    return 0.5 * values * (1.0 + jnp.tanh(gelu_inner(values)))


def gelu_both(values):
    square = values * values
    bend = jnp.tanh(0.7978845608028654 * values * (1.0 + 0.044715 * square))
    half = 0.5 * (1.0 + bend)
    slope = 0.7978845608028654 * (1.0 + 3.0 * 0.044715 * square)
    return values * half, half + 0.5 * values * (1.0 - bend * bend) * slope


def fill_mask(row, mask_ref):
    row = row.astype(F32)
    column = jnp.transpose(jnp.broadcast_to(row, (8, SEQ)))[:, 0:1]
    for step in range(SEQ // 128):
        lanes = slice(step * 128, (step + 1) * 128)
        mask_ref[:, lanes] = jnp.where(column == row[:, lanes], 1.0, 0.0).astype(BF16)


def weights_of(scores, mask, careful):
    if not careful:
        return jnp.exp2(scores).astype(BF16) * mask
    allowed = mask.astype(F32) > 0.5
    scores = jnp.where(allowed, scores, MASKED)
    highest = jnp.max(scores, axis=0, keepdims=True)
    return jnp.exp2(scores - highest).astype(BF16)


def frozen_kernel(
    segment_ref,
    x_ref,
    before_ref,
    middle_ref,
    tap_t_ref,
    wq_hbm,
    wk_hbm,
    wv_hbm,
    wo_hbm,
    we_hbm,
    wr_hbm,
    top_ref,
    tap_ref,
    wq_ref,
    wk_ref,
    wv_ref,
    wo_ref,
    we_ref,
    wr_ref,
    copied,
    mask_ref,
    normed_ref,
    q_ref,
    k_ref,
    v_ref,
    ctx_ref,
    wv_t_ref,
):
    width = x_ref.shape[1]
    heads = width // HEAD
    padded = v_ref.shape[1]

    starting = pl.program_id(0) == 0
    copies = [
        pltpu.make_async_copy(source, target, copied.at[i])
        for i, (source, target) in enumerate(
            (
                (wq_hbm, wq_ref),
                (wk_hbm, wk_ref),
                (wv_hbm, wv_ref),
                (wo_hbm, wo_ref),
                (we_hbm, we_ref),
                (wr_hbm, wr_ref),
            )
        )
    ]

    @pl.when(starting)
    def _():
        for copy in copies:
            copy.start()
        v_ref[:, HEAD:padded] = jnp.ones((heads, padded - HEAD, SEQ), BF16)

    here = lax.axis_index("side") * pl.num_programs(0) + pl.program_id(0)
    fill_mask(segment_ref[here], mask_ref)
    base = x_ref[...].astype(F32)
    factor = lax.rsqrt(jnp.mean(base * base, axis=-1, keepdims=True) + EPS)
    normed_ref[...] = (base * factor * before_ref[...][None]).astype(BF16)
    member = lax.broadcasted_iota(jnp.int32, (width, 128), 0) // HEAD
    member = jnp.where(member == lax.broadcasted_iota(jnp.int32, (width, 128), 1), 1.0, 0.0).astype(BF16)

    def largest(values):
        wide = values.astype(F32)
        return jnp.max(dot((wide * wide).astype(BF16), member), axis=0, keepdims=True)

    @pl.when(starting)
    def _():
        for copy in copies[0:3]:
            copy.wait()
        wv_t_ref[...] = jnp.transpose(wv_ref[...])

    q = (dot(normed_ref[...], wq_ref[...]) * (HEAD**-0.5 * LOG2E)).astype(BF16)
    q_ref[...] = q
    q_top = largest(q)
    k = dot(normed_ref[...], wk_ref[...]).astype(BF16)
    k_ref[...] = k
    bound = jnp.max(q_top * largest(k)) * 1.1
    safe = bound <= SAFE * SAFE
    v = dot(wv_t_ref[...], normed_ref[...], NT).astype(BF16)
    for head in range(heads):
        v_ref[head, 0:HEAD] = v[head * HEAD : (head + 1) * HEAD]

    def attend(careful, tile, together):
        def one(pair, turn, start):
            lanes = pl.ds(start, tile)
            both = pl.ds(pl.multiple_of(pair * 2 * HEAD, 2 * HEAD), 2 * HEAD)
            cols = slice(turn * HEAD, (turn + 1) * HEAD)
            scores = dot(k_ref[:, both][:, cols], q_ref[lanes, both][:, cols], NT)
            probs = weights_of(scores, mask_ref[:, lanes], careful)
            mixed = dot(v_ref[2 * pair + turn], probs)
            rows = pl.ds(pl.multiple_of((2 * pair + turn) * HEAD, HEAD), HEAD)
            ctx_ref[rows, lanes] = (mixed[0:HEAD] / mixed[HEAD : HEAD + 1]).astype(BF16)

        def step(group, carry):
            for pair in range(together):
                for turn in range(2):
                    for i in range(SEQ // tile):
                        one(group * together + pair, turn, i * tile)
            return carry

        lax.fori_loop(0, heads // 2 // together, step, 0)

    pl.when(safe)(lambda: attend(False, TILE, PAIRS))
    pl.when(jnp.logical_not(safe))(lambda: attend(True, TILE, 1))

    @pl.when(starting)
    def _():
        for copy in copies[3:6]:
            copy.wait()

    chunk = 1024
    hidden = we_ref.shape[1]
    piece = 768

    def feed_forward(part, carry):
        rows = pl.ds(pl.multiple_of(part * chunk, chunk), chunk)
        middle = x_ref[rows].astype(F32) + dot(ctx_ref[:, rows], wo_ref[...], TN)
        scale = lax.rsqrt(jnp.mean(middle * middle, axis=-1, keepdims=True) + EPS)
        normed = (middle * scale * middle_ref[...][None]).astype(BF16)
        total = middle
        for j in range(hidden // piece):
            cols = slice(j * piece, (j + 1) * piece)
            expanded = gelu(dot(normed, we_ref[:, cols])).astype(BF16)
            total = total + dot(expanded, wr_ref[cols])
        top = total.astype(BF16)
        top_ref[rows] = top
        tap_ref[:, rows] = dot(tap_t_ref[...], top, NT).astype(BF16)
        return carry

    lax.fori_loop(0, SEQ // chunk, feed_forward, 0)


def whole(array):
    shape = array.shape
    return pl.BlockSpec(shape, lambda i: (0,) * len(shape), pipeline_mode=pl.Buffered(1))


def frozen_block(segment, x, before, middle, wq, wk, wv, wo, we, wr, tap_t):
    tokens, width = x.shape
    heads = width // HEAD
    side = tap_t.shape[0]
    return pl.pallas_call(
        frozen_kernel,
        grid=(tokens // SEQ,),
        in_specs=[
            whole(segment),
            pl.BlockSpec((SEQ, width), lambda i: (i, 0)),
            *map(whole, (before, middle, tap_t)),
            *[pl.BlockSpec(memory_space=pl.ANY)] * 6,
        ],
        out_specs=[
            pl.BlockSpec((SEQ, width), lambda i: (i, 0)),
            pl.BlockSpec((side, SEQ), lambda i: (0, i)),
        ],
        out_shape=[
            jax.ShapeDtypeStruct((tokens, width), BF16),
            jax.ShapeDtypeStruct((side, tokens), BF16),
        ],
        scratch_shapes=[
            *[pltpu.VMEM(w.shape, BF16) for w in (wq, wk, wv, wo, we, wr)],
            pltpu.SemaphoreType.DMA((6,)),
            pltpu.VMEM((SEQ, SEQ), BF16),
            pltpu.VMEM((SEQ, width), BF16),
            pltpu.VMEM((SEQ, width), BF16),
            pltpu.VMEM((SEQ, width), BF16),
            pltpu.VMEM((heads, HEAD + 16, SEQ), BF16),
            pltpu.VMEM((width, SEQ), BF16),
            pltpu.VMEM((width, width), BF16),
        ],
        compiler_params=pltpu.CompilerParams(vmem_limit_bytes=60 << 20),
        name="frozen_block",
    )(segment, x, before, middle, tap_t, wq, wk, wv, wo, we, wr)


def outer_rows(left, right):
    return [left[e : e + 1] * right for e in range(SIDE_HEAD)]


def pack_kernel(expand_ref, q_ref, k_ref, v_ref, output_ref, reduce_ref, packed_ref):
    side, half = expand_ref.shape
    packed_ref[0:side] = expand_ref[:, 0:side]
    packed_ref[side : 2 * side] = expand_ref[:, side:half]
    at = half
    for ref in (q_ref, k_ref, v_ref, output_ref, reduce_ref):
        packed_ref[at : at + ref.shape[0]] = ref[...]
        at += ref.shape[0]


def side_kernel(
    index_ref,
    segment_ref,
    tap_ref,
    stream_ref,
    up_ref,
    top_ref,
    table_ref,
    before_ref,
    middle_ref,
    own_ref,
    other_ref,
    out_ref,
    stream_grad_ref,
    keep_ref,
    send_ref,
    tap_grad_ref,
    qkv_grad_ref,
    out_grad_ref,
    expand_grad_ref,
    reduce_grad_ref,
    small_ref,
    bundle_ref,
    mask_ref,
    w_ref,
    we_ref,
    wo_ref,
    wr_ref,
    e_ref,
    qkv_ref,
    q16_ref,
    k16_ref,
    rows_ref,
    moment_ref,
    ctx_ref,
    dctx_ref,
    dqkv_ref,
):
    side = tap_ref.shape[0]
    heads = side // SIDE_HEAD
    local = side // 2
    hidden = we_ref.shape[1]
    half = hidden // 2

    @pl.when(pl.program_id(0) == 0)
    def _():
        for turn, ref in ((0, own_ref), (1, other_ref)):
            we_ref[:, turn * half : turn * half + side] = ref[0:side]
            we_ref[:, turn * half + side : (turn + 1) * half] = ref[side:half]
            at = half
            w_ref[turn * 3 * local : (turn + 1) * 3 * local] = ref[at : at + 3 * local]
            at += 3 * local
            wo_ref[turn * local : (turn + 1) * local] = ref[at : at + local]
            at += local
            wr_ref[turn * half : (turn + 1) * half] = ref[at : at + half]
        tap_grad_ref[...] = jnp.zeros_like(tap_grad_ref)
        qkv_grad_ref[...] = jnp.zeros_like(qkv_grad_ref)
        out_grad_ref[...] = jnp.zeros_like(out_grad_ref)
        expand_grad_ref[...] = jnp.zeros_like(expand_grad_ref)
        reduce_grad_ref[...] = jnp.zeros_like(reduce_grad_ref)
        small_ref[...] = jnp.zeros_like(small_ref)

    here = lax.axis_index("side") * pl.num_programs(0) + pl.program_id(0)
    fill_mask(segment_ref[here], mask_ref)
    logits = table_ref[pl.ds(index_ref[0], 1), :]
    stacked = jnp.concatenate(
        [
            jnp.broadcast_to(jax.nn.sigmoid(logits), (8, side)),
            jnp.broadcast_to(before_ref[...], (8, side)),
            jnp.broadcast_to(middle_ref[...], (8, side)),
        ],
        axis=0,
    )
    columns = jnp.transpose(stacked)
    gate, before, middle = columns[:, 0:1], columns[:, 8:9], columns[:, 16:17]

    def head_rows(kind, head):
        start = (head // (heads // 2)) * 3 * local + kind * local + (head % (heads // 2)) * SIDE_HEAD
        return pl.ds(pl.multiple_of(start, SIDE_HEAD), SIDE_HEAD)

    tap = tap_ref[...].astype(F32)
    stream = stream_ref[...].astype(F32)
    mixed = gate * tap + (1.0 - gate) * stream
    factor1 = lax.rsqrt(jnp.mean(mixed * mixed, axis=0, keepdims=True) + EPS)
    n1 = (mixed * factor1 * before).astype(BF16)
    qkv_ref[...] = dot(w_ref[...], n1)

    zeros8 = jnp.zeros((SIDE_HEAD, SEQ), F32)
    ones8 = jnp.ones((SIDE_HEAD, SEQ), F32)

    def prepare(head, bound):
        q = qkv_ref[head_rows(0, head)] * (SIDE_HEAD**-0.5 * LOG2E)
        q = q.astype(BF16).astype(F32)
        k = qkv_ref[head_rows(1, head)].astype(BF16).astype(F32)
        v = qkv_ref[head_rows(2, head)].astype(BF16).astype(F32)
        qkv_ref[head_rows(0, head)] = q
        qkv_ref[head_rows(1, head)] = k
        qkv_ref[head_rows(2, head)] = v
        q16_ref[head] = jnp.concatenate([q, zeros8], axis=0).astype(BF16)
        k16_ref[head] = jnp.concatenate([k, zeros8], axis=0).astype(BF16)
        rows = [v, ones8, k, zeros8] + outer_rows(v, k)
        rows_ref[head] = jnp.concatenate(rows, axis=0).astype(BF16)
        return jnp.maximum(
            bound,
            jnp.max(jnp.sum(q * q, axis=0, keepdims=True), axis=1, keepdims=True)
            * jnp.max(jnp.sum(k * k, axis=0, keepdims=True), axis=1, keepdims=True),
        )

    bound = lax.fori_loop(0, heads, prepare, jnp.zeros((1, 1), F32))
    safe = jnp.max(bound) * 1.1 <= SAFE * SAFE

    def attend(careful, tile):
        def one(head, start):
            at = pl.multiple_of(head * SIDE_HEAD, SIDE_HEAD)
            lanes = pl.ds(start, tile)
            scores = dot(k16_ref[head], q16_ref[head, :, lanes], TN)
            probs = weights_of(scores, mask_ref[:, lanes], careful)
            e_ref[head, :, lanes] = probs
            found = dot(rows_ref[head], probs)
            inverse = 1.0 / found[8:16]
            ctx_ref[pl.ds(at, SIDE_HEAD), lanes] = found[0:8] * inverse
            moment_ref[head, 8:16, lanes] = inverse
            moment_ref[head, 16:24, lanes] = found[16:24] * inverse
            for e in range(SIDE_HEAD):
                low = 32 + e * SIDE_HEAD
                moment_ref[head, low : low + 8, lanes] = found[low : low + 8] * inverse

        together = 1 if careful else GROUP

        def step(group, carry):
            for turn in range(together):
                for i in range(SEQ // tile):
                    one(group * together + turn, i * tile)
            return carry

        lax.fori_loop(0, heads // together, step, 0)

    pl.when(safe)(lambda: attend(False, TILE))
    pl.when(jnp.logical_not(safe))(lambda: attend(True, TILE))

    ctx = ctx_ref[...].astype(BF16)
    res1 = mixed + dot(wo_ref[...], ctx, TN)
    factor2 = lax.rsqrt(jnp.mean(res1 * res1, axis=0, keepdims=True) + EPS)
    z = res1 * factor2
    n2 = (z * middle).astype(BF16)
    pre = dot(we_ref[...], n2, TN)
    act, slope = gelu_both(pre)
    act = act.astype(BF16)
    result = res1 + dot(wr_ref[...], act, TN)
    out_ref[...] = result.astype(BF16)

    low_up = up_ref[...]
    up = low_up.astype(F32)
    reduce_grad_ref[...] += dot(low_up, act, NT)
    dpre = (dot(wr_ref[...], low_up) * slope).astype(BF16)
    expand_grad_ref[...] += dot(n2, dpre, NT)
    dn2 = dot(we_ref[...], dpre)
    middle_grad = jnp.sum(dn2 * z, axis=1, keepdims=True)
    u = dn2 * middle
    spread = jnp.mean(u * res1, axis=0, keepdims=True)
    dres1 = up + factor2 * u - z * (factor2 * factor2 * spread)
    low_dres = dres1.astype(BF16)
    out_grad_ref[...] += dot(low_dres, ctx, NT)
    dctx_ref[...] = dot(wo_ref[...], low_dres).astype(BF16).astype(F32)

    def prepare_back(head, carry):
        at = pl.multiple_of(head * SIDE_HEAD, SIDE_HEAD)
        q = qkv_ref[head_rows(0, head)]
        dctx = dctx_ref[pl.ds(at, SIDE_HEAD)]
        inverse = moment_ref[head, 8:16]
        inner = jnp.sum(dctx * ctx_ref[pl.ds(at, SIDE_HEAD)], axis=0, keepdims=True)
        dq = -inner * moment_ref[head, 16:24]
        for e in range(SIDE_HEAD):
            low = 32 + e * SIDE_HEAD
            dq = dq + dctx[e : e + 1] * moment_ref[head, low : low + 8]
        dqkv_ref[head_rows(0, head)] = dq * SIDE_HEAD**-0.5
        scaled = dctx * inverse
        rows = [scaled, zeros8, (inner * inverse) * q, zeros8] + outer_rows(scaled, q)
        rows_ref[head] = jnp.concatenate(rows, axis=0).astype(BF16)
        return carry

    lax.fori_loop(0, heads, prepare_back, 0)

    def back(head):
        found = dot(rows_ref[head], e_ref[head], NT)
        v = qkv_ref[head_rows(2, head)]
        dk = -found[16:24]
        for e in range(SIDE_HEAD):
            low = 32 + e * SIDE_HEAD
            dk = dk + v[e : e + 1] * found[low : low + 8]
        dqkv_ref[head_rows(1, head)] = dk * (1.0 / LOG2E)
        dqkv_ref[head_rows(2, head)] = found[0:8]

    def back_group(group, carry):
        for turn in range(GROUP):
            back(group * GROUP + turn)
        return carry

    lax.fori_loop(0, heads // GROUP, back_group, 0)

    dqkv = dqkv_ref[...].astype(BF16)
    qkv_grad_ref[...] += dot(n1, dqkv, NT)
    dn1 = dot(w_ref[...], dqkv, TN)
    unit = mixed * factor1
    before_grad = jnp.sum(dn1 * unit, axis=1, keepdims=True)
    u = dn1 * before
    spread = jnp.mean(u * mixed, axis=0, keepdims=True)
    dmixed = dres1 + factor1 * u - unit * (factor1 * factor1 * spread)
    logit = jnp.sum(dmixed * (tap - stream), axis=1, keepdims=True) * gate * (1.0 - gate)
    small_ref[...] += jnp.concatenate(
        [logit, before_grad, middle_grad, jnp.zeros((side, 5), F32)], axis=1
    )
    tap_grad_ref[...] += dot((gate * dmixed).astype(BF16), top_ref[...])
    stream_grad_ref[...] = ((1.0 - gate) * dmixed).astype(BF16)

    @pl.when(pl.program_id(0) == pl.num_programs(0) - 1)
    def _():
        for turn in range(2):
            bundle_ref[turn] = jnp.concatenate(
                [
                    expand_grad_ref[:, turn * half : (turn + 1) * half],
                    reduce_grad_ref[:, turn * half : (turn + 1) * half],
                    qkv_grad_ref[:, turn * 3 * local : (turn + 1) * 3 * local],
                    out_grad_ref[:, turn * local : (turn + 1) * local],
                    small_ref[...],
                    jnp.zeros((side, bundle_ref.shape[2] - 2 * half - 4 * local - 8), F32),
                ],
                axis=1,
            )
        place = lax.axis_index("dp")
        me = (place % 2, (place // 2) % 2, lax.axis_index("side"))
        fourth = side // 4
        width = tap_grad_ref.shape[1]
        for core in range(2):
            for x in range(2):
                part = 2 * (me[0] ^ core) + (me[1] ^ x)
                lines = pl.ds(pl.multiple_of(part * fourth, 8), fourth)
                for turn in range(2):
                    first = (me[2] ^ turn) * (width // 2)
                    pieces = [
                        tap_grad_ref[lines, pl.ds(pl.multiple_of(first + j * 128, 128), 128)]
                        for j in range(width // 256)
                    ] + [
                        bundle_ref[turn, lines, j * 128 : (j + 1) * 128]
                        for j in range(bundle_ref.shape[2] // 128)
                    ]
                    block = jnp.concatenate(pieces, axis=0).astype(BF16)
                    (send_ref if core else keep_ref)[2 * x + turn] = block


def side_block(index, segment, tap, stream, up, top, table, before, middle, own, other):
    side, tokens = stream.shape
    width = top.shape[1]
    heads = side // SIDE_HEAD
    hidden = own.shape[0] - 2 * side
    bundle = -(-(hidden + 2 * side + 8) // 128) * 128
    block = (side // 4) * (width // 256 + bundle // 128)

    def lanes(height):
        return pl.BlockSpec((height, SEQ), lambda i: (0, i))

    packed = pl.BlockSpec((4, block, 128), lambda i: (0, 0, 0))
    return pl.pallas_call(
        side_kernel,
        grid=(tokens // SEQ,),
        in_specs=[
            pl.BlockSpec(memory_space=pltpu.SMEM),
            whole(segment),
            lanes(side),
            lanes(side),
            lanes(side),
            pl.BlockSpec((SEQ, width), lambda i: (i, 0)),
            *map(whole, (table, before, middle, own, other)),
        ],
        out_specs=[lanes(side), lanes(side), packed, packed],
        out_shape=[
            jax.ShapeDtypeStruct((side, tokens), BF16),
            jax.ShapeDtypeStruct((side, tokens), BF16),
            jax.ShapeDtypeStruct((4, block, 128), BF16),
            jax.ShapeDtypeStruct((4, block, 128), BF16),
        ],
        scratch_shapes=[
            pltpu.VMEM((side, width), F32),
            pltpu.VMEM((side, 3 * side), F32),
            pltpu.VMEM((side, side), F32),
            pltpu.VMEM((side, hidden), F32),
            pltpu.VMEM((side, hidden), F32),
            pltpu.VMEM((side, 8), F32),
            pltpu.VMEM((2, side, bundle), F32),
            pltpu.VMEM((SEQ, SEQ), BF16),
            pltpu.VMEM((3 * side, side), BF16),
            pltpu.VMEM((side, hidden), BF16),
            pltpu.VMEM((side, side), BF16),
            pltpu.VMEM((hidden, side), BF16),
            pltpu.VMEM((heads, SEQ, SEQ), BF16),
            pltpu.VMEM((3 * side, SEQ), F32),
            pltpu.VMEM((heads, 16, SEQ), BF16),
            pltpu.VMEM((heads, 16, SEQ), BF16),
            pltpu.VMEM((heads, ROWS, SEQ), BF16),
            pltpu.VMEM((heads, ROWS, SEQ), F32),
            pltpu.VMEM((side, SEQ), F32),
            pltpu.VMEM((side, SEQ), F32),
            pltpu.VMEM((3 * side, SEQ), F32),
        ],
        compiler_params=pltpu.CompilerParams(vmem_limit_bytes=60 << 20),
        name="side_block",
    )(index, segment, tap, stream, up, top, table, before, middle, own, other)


def unpack_kernel(
    index_ref,
    near_ref,
    far_ref,
    tap_ref,
    gate_ref,
    before_ref,
    middle_ref,
    q_ref,
    k_ref,
    v_ref,
    output_ref,
    expand_ref,
    reduce_ref,
    bundle_ref,
):
    side, width = tap_ref.shape
    half = expand_ref.shape[1]
    local = side // 2
    fourth = side // 4
    taps = width // 256
    tiles = bundle_ref.shape[1] // 128
    block = fourth * (taps + tiles)
    place = lax.axis_index("dp")
    me = (place % 2, (place // 2) % 2, lax.axis_index("side"))
    for core in range(2):
        held = (far_ref if core else near_ref)[...].astype(F32)
        for x in range(2):
            part = 2 * (me[0] ^ core) + (me[1] ^ x)
            lines = pl.ds(pl.multiple_of(part * fourth, 8), fourth)
            for turn in range(2):
                at = 2 * block + x * taps * fourth if turn else x * block
                first = (me[2] ^ turn) * (width // 2)
                for j in range(taps):
                    cols = pl.ds(pl.multiple_of(first + j * 128, 128), 128)
                    tap_ref[lines, cols] = held[at + j * fourth : at + (j + 1) * fourth]
            for j in range(tiles):
                at = x * block + (taps + j) * fourth
                bundle_ref[lines, j * 128 : (j + 1) * 128] = held[at : at + fourth]
    expand_ref[...] = bundle_ref[:, 0:half]
    reduce_ref[...] = jnp.transpose(bundle_ref[:, half : 2 * half])
    rest = jnp.transpose(bundle_ref[:, 2 * half : 2 * half + 4 * local + 8])
    q_ref[...] = rest[0:local]
    k_ref[...] = rest[local : 2 * local]
    v_ref[...] = rest[2 * local : 3 * local]
    output_ref[...] = rest[3 * local : 4 * local]
    small = rest[4 * local : 4 * local + 8]
    picked = lax.broadcasted_iota(jnp.int32, gate_ref.shape, 0) == index_ref[0]
    gate_ref[...] = jnp.where(picked, small[0:1], 0.0)
    before_ref[...] = small[1:2]
    middle_ref[...] = small[2:3]


def exchange(values, dp, side, dp_size):
    pairs = [
        (2 * i + s, 2 * (i ^ dp) + (s ^ side)) for i in range(dp_size) for s in range(2)
    ]
    return lax.ppermute(values, ("dp", "side"), pairs)


def add(*values):
    return functools.reduce(lambda a, b: a + b, [v.astype(F32) for v in values]).astype(BF16)


def shards(
    dp_size,
    backbone_in,
    segment_ids,
    gate_index,
    norm_before,
    norm_middle,
    frozen_query,
    frozen_key,
    frozen_value,
    frozen_output,
    frozen_expand,
    frozen_reduce,
    tap_weight,
    gate_table,
    side_stream,
    ladder_before,
    ladder_middle,
    ladder_query,
    ladder_key,
    ladder_value,
    ladder_output,
    ladder_expand,
    ladder_reduce,
    cotangent,
):
    side = side_stream.shape[1]
    width = tap_weight.shape[0]
    local = side // 2
    half = ladder_expand.shape[1]
    swap = functools.partial(exchange, dp_size=dp_size)
    own = pl.pallas_call(
        pack_kernel,
        out_shape=jax.ShapeDtypeStruct((2 * half + 4 * local, side), BF16),
        name="pack_weights",
    )(ladder_expand, ladder_query.T, ladder_key.T, ladder_value.T, ladder_output, ladder_reduce)
    other = swap(own, 0, 1)
    segment = segment_ids.reshape(-1, 1, SEQ)
    top, tap = frozen_block(
        segment,
        backbone_in,
        norm_before,
        norm_middle,
        frozen_query,
        frozen_key,
        frozen_value,
        frozen_output,
        frozen_expand,
        frozen_reduce,
        tap_weight.T,
    )
    result, stream_grad, keep, send = side_block(
        gate_index,
        segment,
        tap,
        side_stream.T,
        cotangent.T,
        top,
        gate_table,
        ladder_before[None],
        ladder_middle[None],
        own,
        other,
    )
    block = keep.shape[1]
    taps = (side // 4) * (width // 256)
    quad = add(keep, swap(send, 1, 0))
    mine = add(quad[0], swap(quad[1], 0, 1), swap(quad[2], 2, 0), swap(quad[3], 2, 1))
    bit = 4
    while bit < dp_size:
        mine = add(mine, swap(mine, bit, 0))
        bit *= 2
    near = jnp.concatenate(
        [mine, swap(mine, 2, 0), swap(mine[:taps], 0, 1), swap(mine[:taps], 2, 1)], axis=0
    )
    far = swap(near, 1, 0)
    shape = functools.partial(jax.ShapeDtypeStruct, dtype=F32)
    tap_sum, gate_sum, before_sum, middle_sum, q_sum, k_sum, v_sum, out_sum, expand_sum, reduce_sum = pl.pallas_call(
        unpack_kernel,
        in_specs=[
            pl.BlockSpec(memory_space=pltpu.SMEM),
            pl.BlockSpec(memory_space=pltpu.VMEM),
            pl.BlockSpec(memory_space=pltpu.VMEM),
        ],
        out_shape=[
            shape((side, width)),
            shape(gate_table.shape),
            shape((1, side)),
            shape((1, side)),
            shape((local, side)),
            shape((local, side)),
            shape((local, side)),
            shape((local, side)),
            shape((side, half)),
            shape((half, side)),
        ],
        scratch_shapes=[pltpu.VMEM((side, (block - taps) // (side // 4) * 128), F32)],
        compiler_params=pltpu.CompilerParams(vmem_limit_bytes=8 << 20),
        name="unpack_gradients",
    )(gate_index, near, far)
    return (
        result.T,
        stream_grad.T,
        tap_sum.T,
        gate_sum,
        before_sum[0],
        middle_sum[0],
        q_sum.T,
        k_sum.T,
        v_sum.T,
        out_sum,
        expand_sum,
        reduce_sum,
    )


def solution(mesh):
    rows = P(("dp", "side"), None)
    placed = (
        rows,
        P("dp"),
        *([P()] * 11),
        rows,
        P(),
        P(),
        P(None, "side"),
        P(None, "side"),
        P(None, "side"),
        P("side", None),
        P(None, "side"),
        P("side", None),
        rows,
    )
    return jax.shard_map(
        functools.partial(shards, mesh.shape["dp"]),
        mesh=mesh,
        in_specs=placed,
        out_specs=(
            rows,
            rows,
            P(),
            P(),
            P(),
            P(),
            P(None, "side"),
            P(None, "side"),
            P(None, "side"),
            P("side", None),
            P(None, "side"),
            P("side", None),
        ),
        check_vma=False,
    )
```

profile of v0, /device:TPU:0, one launch (start us, length us, event | category | flops | bytes accessed | tf_op | source)
XLA Modules:
  0.0 154.5 jit_solution(11329551870796273492)
XLA Ops:
  0.6 1.6 %pack_weights.1.own_ref = bf16[576,96]{1,0:T(8,128)(2,1)} custom-call(bf16[96,192]{1,0:T(8,128)(2,1)} %expand_ref.1, bf16[48,96]{1,0:T(8,128)(2,1)} %bitcast.33, bf16[48,96]{1,0:T(8,128)(2,1)} %bitcast.34, bf16[48,96]{1,0:T(8,128)(2,1)} %bitcast.35, bf16[48,96]{1,0:T(8,128)(2,1)} %output_ref.1, bf16[192,96]{1,0:T(8,128)(2,1)} %reduce_ref.1), custom_call_target="tpu_custom_call" | custom-call | tf_op jit(solution)/shard_map/pack_weights/pallas_call | solution.py:659
  2.3 3.0 %collective-permute-start = (bf16[576,96]{1,0:T(8,128)(2,1)}, bf16[576,96]{1,0:T(8,128)(2,1)S(1)}, u32[]{:S(2)}, u32[]{:S(2)}) collective-permute-start(bf16[576,96]{1,0:T(8,128)(2,1)} %pack_weights.1.own_ref), channel_id=1, source_target_pairs={{0,1},{1,0},{2,3},{3,2},{4,5},{5,4},{6,7},{7,6},{8,9},{9,8},{10,11... | collective-permute-start | bytes 331784 | tf_op jit(solution)/shard_map/ppermute | solution.py:621
  5.9 65.9 %frozen_block.1 = (bf16[2048,768]{1,0:T(8,128)(2,1)}, bf16[96,2048]{1,0:T(8,128)(2,1)}) custom-call(s32[4,1,1024]{2,1,0:T(1,128)} %bitcast.31, bf16[2048,768]{1,0:T(8,128)(2,1)} %x_ref.1, f32[768]{0:T(1024)} %before_ref.1, f32[768]{0:T(1024)} %middle_ref.1, bf16[96,768]{1,0:T(8,128)(2,1)} %bitcast.30, bf16[768,768]{1,0:T(8,128)(2,1)} %wq_hbm.1, ...), custom_call_target="tpu_custom_call" | custom-call | tf_op jit(solution)/shard_map/frozen_block/pallas_call | solution.py:208
  71.8 0.0 collective-permute-done.other_ref
  71.8 0.0 copy-start
  71.8 0.6 copy-done
  72.5 54.8 %side_block.1 = (bf16[96,2048]{1,0:T(8,128)(2,1)}, bf16[96,2048]{1,0:T(8,128)(2,1)}, bf16[4,192,128]{2,1,0:T(8,128)(2,1)}, bf16[4,192,128]{2,1,0:T(8,128)(2,1)}) custom-call(s32[1]{0:T(128)S(6)} %copy.35.index_ref, s32[4,1,1024]{2,1,0:T(1,128)} %bitcast.32, bf16[96,2048]{1,0:T(8,128)(2,1)} %get-tuple-element.28.tap_ref, bf16[96,2048]{1,0:T(8,128)(2,1)} %bitcast.28, ...), custom_call_target="tpu_custom_call" | custom-call | tf_op jit(solution)/shard_map/side_block/pallas_call | solution.py:517
  127.3 0.1 collective-permute-start.1
  127.3 1.6 %collective-permute-done.1 = bf16[4,192,128]{2,1,0:T(8,128)(2,1)S(1)} collective-permute-done((bf16[4,192,128]{2,1,0:T(8,128)(2,1)}, bf16[4,192,128]{2,1,0:T(8,128)(2,1)S(1)}, u32[]{:S(2)}, u32[]{:S(2)}) %collective-permute-start.1) | collective-permute-done | bytes 196640 | tf_op jit(solution)/shard_map/ppermute | solution.py:621
  129.0 1.0 add_convert_fusion
  130.0 0.1 collective-permute-start.2
  130.1 2.9 %collective-permute-start.4 = (bf16[192,128]{1,0:T(8,128)(2,1)S(1)}, bf16[192,128]{1,0:T(8,128)(2,1)S(1)}, u32[]{:S(2)}, u32[]{:S(2)}) collective-permute-start(bf16[192,128]{1,0:T(8,128)(2,1)S(1)} %get-tuple-element.45), channel_id=1, source_target_pairs={{0,5},{1,4},{2,7},{3,6},{4,1},{5,0},{6,3},{7,2},{8,13},{9,12},{10,... | collective-permute-start | bytes 147464 | tf_op jit(solution)/shard_map/ppermute | solution.py:621
  133.0 0.5 collective-permute-start.3
  133.5 1.7 %collective-permute-done.2 = bf16[192,128]{1,0:T(8,128)(2,1)S(1)} collective-permute-done((bf16[192,128]{1,0:T(8,128)(2,1)S(1)}, bf16[192,128]{1,0:T(8,128)(2,1)S(1)}, u32[]{:S(2)}, u32[]{:S(2)}) %collective-permute-start.2) | collective-permute-done | bytes 49184 | tf_op jit(solution)/shard_map/ppermute | solution.py:621
  135.2 0.0 collective-permute-done.4
  135.2 1.9 %collective-permute-done.3 = bf16[192,128]{1,0:T(8,128)(2,1)S(1)} collective-permute-done((bf16[192,128]{1,0:T(8,128)(2,1)S(1)}, bf16[192,128]{1,0:T(8,128)(2,1)S(1)}, u32[]{:S(2)}, u32[]{:S(2)}) %collective-permute-start.3) | collective-permute-done | bytes 49184 | tf_op jit(solution)/shard_map/ppermute | solution.py:621
  137.1 1.6 %collective-permute-start.5 = (bf16[192,128]{1,0:T(8,128)(2,1)S(1)}, bf16[192,128]{1,0:T(8,128)(2,1)S(1)}, u32[]{:S(2)}, u32[]{:S(2)}) collective-permute-start(bf16[192,128]{1,0:T(8,128)(2,1)S(1)} %fusion.2), channel_id=1, source_target_pairs={{0,8},{1,9},{2,10},{3,11},{4,12},{5,13},{6,14},{7,15},{8,0},{9,1},... | collective-permute-start | bytes 147464 | tf_op jit(solution)/shard_map/ppermute | solution.py:621
  138.8 2.5 %collective-permute-done.5 = bf16[192,128]{1,0:T(8,128)(2,1)S(1)} collective-permute-done((bf16[192,128]{1,0:T(8,128)(2,1)S(1)}, bf16[192,128]{1,0:T(8,128)(2,1)S(1)}, u32[]{:S(2)}, u32[]{:S(2)}) %collective-permute-start.5) | collective-permute-done | bytes 49184 | tf_op jit(solution)/shard_map/ppermute | solution.py:621
  141.3 2.7 %collective-permute-start.6 = (bf16[192,128]{1,0:T(8,128)(2,1)S(1)}, bf16[192,128]{1,0:T(8,128)(2,1)S(1)}, u32[]{:S(2)}, u32[]{:S(2)}) collective-permute-start(bf16[192,128]{1,0:T(8,128)(2,1)S(1)} %add_convert_fusion.2), channel_id=1, source_target_pairs={{0,16},{1,17},{2,18},{3,19},{4,20},{5,21},{6,22},{7,23},{8,24},{9,... | collective-permute-start | bytes 147464 | tf_op jit(solution)/shard_map/ppermute | solution.py:621
  144.0 2.4 %collective-permute-done.6 = bf16[192,128]{1,0:T(8,128)(2,1)S(1)} collective-permute-done((bf16[192,128]{1,0:T(8,128)(2,1)S(1)}, bf16[192,128]{1,0:T(8,128)(2,1)S(1)}, u32[]{:S(2)}, u32[]{:S(2)}) %collective-permute-start.6) | collective-permute-done | bytes 49184 | tf_op jit(solution)/shard_map/ppermute | solution.py:621
  146.4 0.6 collective-permute-start.7
  147.0 1.4 collective-permute-start.9
  148.4 1.5 collective-permute-start.8
  149.9 1.7 %collective-permute-done.9 = bf16[72,128]{1,0:T(8,128)(2,1)S(1)} collective-permute-done((bf16[72,128]{1,0:T(8,128)(2,1)S(1)}, bf16[72,128]{1,0:T(8,128)(2,1)S(1)}, u32[]{:S(2)}, u32[]{:S(2)}) %collective-permute-start.9) | collective-permute-done | bytes 18464 | tf_op jit(solution)/shard_map/ppermute | solution.py:621
  151.6 0.5 collective-permute-done.8
  152.2 0.0 collective-permute-done.7
  152.2 0.1 collective-permute-start.10
  152.3 1.3 collective-permute-done.10.far_ref
  153.6 0.9 unpack_gradients.1
  (6 shorter events, 0.1 us)
Async XLA Ops:
  2.3 69.5 %collective-permute-start = (bf16[576,96]{1,0:T(8,128)(2,1)}, bf16[576,96]{1,0:T(8,128)(2,1)S(1)}, u32[]{:S(2)}, u32[]{:S(2)}) collective-permute-start(bf16[576,96]{1,0:T(8,128)(2,1)} %pack_weights.1.own_ref), channel_id=1, source_target_pairs={{0,1},{1,0},{2,3},{3,2},{4,5},{5,4},{6,7},{7,6},{8,9},{9,8},{10,11... | collective-permute-start | bytes 331784 | tf_op jit(solution)/shard_map/ppermute | solution.py:621
  71.8 0.7 copy-start
  127.3 1.7 %collective-permute-start.1 = (bf16[4,192,128]{2,1,0:T(8,128)(2,1)}, bf16[4,192,128]{2,1,0:T(8,128)(2,1)S(1)}, u32[]{:S(2)}, u32[]{:S(2)}) collective-permute-start(bf16[4,192,128]{2,1,0:T(8,128)(2,1)} %get-tuple-element.33), channel_id=1, source_target_pairs={{0,2},{1,3},{2,0},{3,1},{4,6},{5,7},{6,4},{7,5},{8,10},{9,11},{10,... | collective-permute-start | bytes 589832 | tf_op jit(solution)/shard_map/ppermute | solution.py:621
  130.0 5.2 %collective-permute-start.2 = (bf16[192,128]{1,0:T(8,128)(2,1)S(1)}, bf16[192,128]{1,0:T(8,128)(2,1)S(1)}, u32[]{:S(2)}, u32[]{:S(2)}) collective-permute-start(bf16[192,128]{1,0:T(8,128)(2,1)S(1)} %get-tuple-element.44), channel_id=1, source_target_pairs={{0,1},{1,0},{2,3},{3,2},{4,5},{5,4},{6,7},{7,6},{8,9},{9,8},{10,11... | collective-permute-start | bytes 147464 | tf_op jit(solution)/shard_map/ppermute | solution.py:621
  130.1 5.1 %collective-permute-start.4 = (bf16[192,128]{1,0:T(8,128)(2,1)S(1)}, bf16[192,128]{1,0:T(8,128)(2,1)S(1)}, u32[]{:S(2)}, u32[]{:S(2)}) collective-permute-start(bf16[192,128]{1,0:T(8,128)(2,1)S(1)} %get-tuple-element.45), channel_id=1, source_target_pairs={{0,5},{1,4},{2,7},{3,6},{4,1},{5,0},{6,3},{7,2},{8,13},{9,12},{10,... | collective-permute-start | bytes 147464 | tf_op jit(solution)/shard_map/ppermute | solution.py:621
  133.0 4.1 %collective-permute-start.3 = (bf16[192,128]{1,0:T(8,128)(2,1)S(1)}, bf16[192,128]{1,0:T(8,128)(2,1)S(1)}, u32[]{:S(2)}, u32[]{:S(2)}) collective-permute-start(bf16[192,128]{1,0:T(8,128)(2,1)S(1)} %get-tuple-element.46), channel_id=1, source_target_pairs={{0,4},{1,5},{2,6},{3,7},{4,0},{5,1},{6,2},{7,3},{8,12},{9,13},{10,... | collective-permute-start | bytes 147464 | tf_op jit(solution)/shard_map/ppermute | solution.py:621
  137.1 4.2 %collective-permute-start.5 = (bf16[192,128]{1,0:T(8,128)(2,1)S(1)}, bf16[192,128]{1,0:T(8,128)(2,1)S(1)}, u32[]{:S(2)}, u32[]{:S(2)}) collective-permute-start(bf16[192,128]{1,0:T(8,128)(2,1)S(1)} %fusion.2), channel_id=1, source_target_pairs={{0,8},{1,9},{2,10},{3,11},{4,12},{5,13},{6,14},{7,15},{8,0},{9,1},... | collective-permute-start | bytes 147464 | tf_op jit(solution)/shard_map/ppermute | solution.py:621
  141.3 5.1 %collective-permute-start.6 = (bf16[192,128]{1,0:T(8,128)(2,1)S(1)}, bf16[192,128]{1,0:T(8,128)(2,1)S(1)}, u32[]{:S(2)}, u32[]{:S(2)}) collective-permute-start(bf16[192,128]{1,0:T(8,128)(2,1)S(1)} %add_convert_fusion.2), channel_id=1, source_target_pairs={{0,16},{1,17},{2,18},{3,19},{4,20},{5,21},{6,22},{7,23},{8,24},{9,... | collective-permute-start | bytes 147464 | tf_op jit(solution)/shard_map/ppermute | solution.py:621
  146.4 5.8 %collective-permute-start.7 = (bf16[192,128]{1,0:T(8,128)(2,1)S(1)}, bf16[192,128]{1,0:T(8,128)(2,1)S(1)}, u32[]{:S(2)}, u32[]{:S(2)}) collective-permute-start(bf16[192,128]{1,0:T(8,128)(2,1)S(1)} %add_convert_fusion.1), channel_id=1, source_target_pairs={{0,4},{1,5},{2,6},{3,7},{4,0},{5,1},{6,2},{7,3},{8,12},{9,13},{10,... | collective-permute-start | bytes 147464 | tf_op jit(solution)/shard_map/ppermute | solution.py:621
  147.0 4.7 %collective-permute-start.9 = (bf16[72,128]{1,0:T(8,128)(2,1)S(1)}, bf16[72,128]{1,0:T(8,128)(2,1)S(1)}, u32[]{:S(2)}, u32[]{:S(2)}) collective-permute-start(bf16[72,128]{1,0:T(8,128)(2,1)S(1)} %slice.25), channel_id=1, source_target_pairs={{0,5},{1,4},{2,7},{3,6},{4,1},{5,0},{6,3},{7,2},{8,13},{9,12},{10,... | collective-permute-start | bytes 55304 | tf_op jit(solution)/shard_map/ppermute | solution.py:621
  148.4 3.8 %collective-permute-start.8 = (bf16[72,128]{1,0:T(8,128)(2,1)S(1)}, bf16[72,128]{1,0:T(8,128)(2,1)S(1)}, u32[]{:S(2)}, u32[]{:S(2)}) collective-permute-start(bf16[72,128]{1,0:T(8,128)(2,1)S(1)} %slice.25), channel_id=1, source_target_pairs={{0,1},{1,0},{2,3},{3,2},{4,5},{5,4},{6,7},{7,6},{8,9},{9,8},{10,11... | collective-permute-start | bytes 55304 | tf_op jit(solution)/shard_map/ppermute | solution.py:621
  152.2 1.4 collective-permute-start.10
where the time goes:
time: 155 us
  Pallas kernels  123 us (79%)
  starting transfers between devices  14.5 us (9%)
  waiting for transfers between devices  13.7 us (9%)
    pallas_call x1, Pallas kernels, frozen_block(): pl.pallas_call(frozen_kernel, grid=(tokens // SEQ,), in_specs=[whole(segm...  65.9 us
    pallas_call x1, Pallas kernels, side_block(): pl.pallas_call(side_kernel, grid=(tokens // SEQ,), in_specs=[pl.BlockSpec...  54.8 us
    ppermute x11, starting transfers between devices, exchange(): return lax.ppermute(values, ('dp', 'side'), pairs)  14.5 us
    ppermute x11, waiting for transfers between devices, exchange(): return lax.ppermute(values, ('dp', 'side'), pairs)  13.7 us
  transfers between devices with their start and end apart: 11, of which 8 were waited for; matrix products, arithmetic and copies ran while one was open for 0% of the time, Pallas kernels for 43%

commit v1 on v0

--- a/solution.py
+++ b/solution.py
@@ -13,7 +13,8 @@
 EPS = 1e-06
 MASKED = -1e30
 LOG2E = 1.4426950408889634
-SAFE = 64.0
+LEAST = 2.0**-64
+MOST = 2.0**64
 TILE = 512
 ROWS = 96
 GROUP = 4
@@ -52,6 +53,11 @@
     for step in range(SEQ // 128):
         lanes = slice(step * 128, (step + 1) * 128)
         mask_ref[:, lanes] = jnp.where(column == row[:, lanes], 1.0, 0.0).astype(BF16)
+
+
+def note_totals(fine_ref, totals):
+    fine = jnp.logical_and(totals >= LEAST, totals <= MOST)
+    fine_ref[...] = jnp.where(fine, fine_ref[...], 0.0)
 
 
 def weights_of(scores, mask, careful):
@@ -91,6 +97,7 @@
     v_ref,
     ctx_ref,
     wv_t_ref,
+    fine_ref,
 ):
     width = x_ref.shape[1]
     heads = width // HEAD
@@ -113,7 +120,7 @@
 
     @pl.when(starting)
     def _():
-        for copy in copies:
+        for copy in copies[0:3]:
             copy.start()
         v_ref[:, HEAD:padded] = jnp.ones((heads, padded - HEAD, SEQ), BF16)
 
@@ -122,26 +129,16 @@
     base = x_ref[...].astype(F32)
     factor = lax.rsqrt(jnp.mean(base * base, axis=-1, keepdims=True) + EPS)
     normed_ref[...] = (base * factor * before_ref[...][None]).astype(BF16)
-    member = lax.broadcasted_iota(jnp.int32, (width, 128), 0) // HEAD
-    member = jnp.where(member == lax.broadcasted_iota(jnp.int32, (width, 128), 1), 1.0, 0.0).astype(BF16)
-
-    def largest(values):
-        wide = values.astype(F32)
-        return jnp.max(dot((wide * wide).astype(BF16), member), axis=0, keepdims=True)
-
     @pl.when(starting)
     def _():
         for copy in copies[0:3]:
             copy.wait()
+        for copy in copies[3:6]:
+            copy.start()
         wv_t_ref[...] = jnp.transpose(wv_ref[...])
 
-    q = (dot(normed_ref[...], wq_ref[...]) * (HEAD**-0.5 * LOG2E)).astype(BF16)
-    q_ref[...] = q
-    q_top = largest(q)
-    k = dot(normed_ref[...], wk_ref[...]).astype(BF16)
-    k_ref[...] = k
-    bound = jnp.max(q_top * largest(k)) * 1.1
-    safe = bound <= SAFE * SAFE
+    q_ref[...] = (dot(normed_ref[...], wq_ref[...]) * (HEAD**-0.5 * LOG2E)).astype(BF16)
+    k_ref[...] = dot(normed_ref[...], wk_ref[...]).astype(BF16)
     v = dot(wv_t_ref[...], normed_ref[...], NT).astype(BF16)
     for head in range(heads):
         v_ref[head, 0:HEAD] = v[head * HEAD : (head + 1) * HEAD]
@@ -154,6 +151,8 @@
             scores = dot(k_ref[:, both][:, cols], q_ref[lanes, both][:, cols], NT)
             probs = weights_of(scores, mask_ref[:, lanes], careful)
             mixed = dot(v_ref[2 * pair + turn], probs)
+            if not careful:
+                note_totals(fine_ref, mixed[HEAD : HEAD + 8])
             rows = pl.ds(pl.multiple_of((2 * pair + turn) * HEAD, HEAD), HEAD)
             ctx_ref[rows, lanes] = (mixed[0:HEAD] / mixed[HEAD : HEAD + 1]).astype(BF16)
 
@@ -166,8 +165,9 @@
 
         lax.fori_loop(0, heads // 2 // together, step, 0)
 
-    pl.when(safe)(lambda: attend(False, TILE, PAIRS))
-    pl.when(jnp.logical_not(safe))(lambda: attend(True, TILE, 1))
+    fine_ref[...] = jnp.ones_like(fine_ref)
+    attend(False, TILE, PAIRS)
+    pl.when(jnp.min(fine_ref[...]) < 0.5)(lambda: attend(True, TILE, 1))
 
     @pl.when(starting)
     def _():
@@ -232,6 +232,7 @@
             pltpu.VMEM((heads, HEAD + 16, SEQ), BF16),
             pltpu.VMEM((width, SEQ), BF16),
             pltpu.VMEM((width, width), BF16),
+            pltpu.VMEM((8, TILE), F32),
         ],
         compiler_params=pltpu.CompilerParams(vmem_limit_bytes=60 << 20),
         name="frozen_block",
@@ -289,6 +290,7 @@
     ctx_ref,
     dctx_ref,
     dqkv_ref,
+    fine_ref,
 ):
     side = tap_ref.shape[0]
     heads = side // SIDE_HEAD
@@ -342,7 +344,7 @@
     zeros8 = jnp.zeros((SIDE_HEAD, SEQ), F32)
     ones8 = jnp.ones((SIDE_HEAD, SEQ), F32)
 
-    def prepare(head, bound):
+    def prepare(head, carry):
         q = qkv_ref[head_rows(0, head)] * (SIDE_HEAD**-0.5 * LOG2E)
         q = q.astype(BF16).astype(F32)
         k = qkv_ref[head_rows(1, head)].astype(BF16).astype(F32)
@@ -354,14 +356,9 @@
         k16_ref[head] = jnp.concatenate([k, zeros8], axis=0).astype(BF16)
         rows = [v, ones8, k, zeros8] + outer_rows(v, k)
         rows_ref[head] = jnp.concatenate(rows, axis=0).astype(BF16)
-        return jnp.maximum(
-            bound,
-            jnp.max(jnp.sum(q * q, axis=0, keepdims=True), axis=1, keepdims=True)
-            * jnp.max(jnp.sum(k * k, axis=0, keepdims=True), axis=1, keepdims=True),
-        )
-
-    bound = lax.fori_loop(0, heads, prepare, jnp.zeros((1, 1), F32))
-    safe = jnp.max(bound) * 1.1 <= SAFE * SAFE
+        return carry
+
+    lax.fori_loop(0, heads, prepare, 0)
 
     def attend(careful, tile):
         def one(head, start):
@@ -369,8 +366,10 @@
             lanes = pl.ds(start, tile)
             scores = dot(k16_ref[head], q16_ref[head, :, lanes], TN)
             probs = weights_of(scores, mask_ref[:, lanes], careful)
-            e_ref[head, :, lanes] = probs
+            e_ref[head, lanes, :] = jnp.transpose(probs)
             found = dot(rows_ref[head], probs)
+            if not careful:
+                note_totals(fine_ref, found[8:16])
             inverse = 1.0 / found[8:16]
             ctx_ref[pl.ds(at, SIDE_HEAD), lanes] = found[0:8] * inverse
             moment_ref[head, 8:16, lanes] = inverse
@@ -389,8 +388,9 @@
 
         lax.fori_loop(0, heads // together, step, 0)
 
-    pl.when(safe)(lambda: attend(False, TILE))
-    pl.when(jnp.logical_not(safe))(lambda: attend(True, TILE))
+    fine_ref[...] = jnp.ones_like(fine_ref)
+    attend(False, TILE)
+    pl.when(jnp.min(fine_ref[...]) < 0.5)(lambda: attend(True, TILE))
 
     ctx = ctx_ref[...].astype(BF16)
     res1 = mixed + dot(wo_ref[...], ctx, TN)
@@ -436,7 +436,7 @@
     lax.fori_loop(0, heads, prepare_back, 0)
 
     def back(head):
-        found = dot(rows_ref[head], e_ref[head], NT)
+        found = dot(rows_ref[head], e_ref[head])
         v = qkv_ref[head_rows(2, head)]
         dk = -found[16:24]
         for e in range(SIDE_HEAD):
@@ -555,6 +555,7 @@
             pltpu.VMEM((side, SEQ), F32),
             pltpu.VMEM((side, SEQ), F32),
             pltpu.VMEM((3 * side, SEQ), F32),
+            pltpu.VMEM((8, TILE), F32),
         ],
         compiler_params=pltpu.CompilerParams(vmem_limit_bytes=60 << 20),
         name="side_block",

time: 155 us -> 149 us (0.961)
  Pallas kernels: 123 us -> 117 us
    pallas_call x1, Pallas kernels: 54.8 us -> 50.4 us  [side_block(): pl.pallas_call(side_kernel, grid=(tokens // SEQ,), in_specs=[pl.BlockSpec...]
    pallas_call x1, Pallas kernels: 65.9 us -> 64.2 us  [frozen_block(): pl.pallas_call(frozen_kernel, grid=(tokens // SEQ,), in_specs=[whole(segm...]
where the time goes in v1:
time: 149 us; the launch traced here: 148 us
  Pallas kernels  117 us (79%)
  starting transfers between devices  14.5 us (10%)
  waiting for transfers between devices  13.7 us (9%)
    pallas_call x1, Pallas kernels, frozen_block(): pl.pallas_call(frozen_kernel, grid=(tokens // SEQ,), in_specs=[whole(segm...  64.2 us
    pallas_call x1, Pallas kernels, side_block(): pl.pallas_call(side_kernel, grid=(tokens // SEQ,), in_specs=[pl.BlockSpec...  50.4 us
    ppermute x11, starting transfers between devices, exchange(): return lax.ppermute(values, ('dp', 'side'), pairs)  14.5 us
    ppermute x11, waiting for transfers between devices, exchange(): return lax.ppermute(values, ('dp', 'side'), pairs)  13.7 us
  transfers between devices with their start and end apart: 11, of which 8 were waited for; matrix products, arithmetic and copies ran while one was open for 0% of the time, Pallas kernels for 43%

profile of v1, /device:TPU:0, one launch (start us, length us, event | category | flops | bytes accessed | tf_op | source)
XLA Modules:
  0.0 148.4 jit_solution(17799880378882631176)
XLA Ops:
  0.6 1.6 %pack_weights.1.own_ref = bf16[576,96]{1,0:T(8,128)(2,1)} custom-call(bf16[96,192]{1,0:T(8,128)(2,1)} %expand_ref.1, bf16[48,96]{1,0:T(8,128)(2,1)} %bitcast.33, bf16[48,96]{1,0:T(8,128)(2,1)} %bitcast.34, bf16[48,96]{1,0:T(8,128)(2,1)} %bitcast.35, bf16[48,96]{1,0:T(8,128)(2,1)} %output_ref.1, bf16[192,96]{1,0:T(8,128)(2,1)} %reduce_ref.1), custom_call_target="tpu_custom_call" | custom-call | tf_op jit(solution)/shard_map/pack_weights/pallas_call | solution.py:660
  2.3 3.0 %collective-permute-start = (bf16[576,96]{1,0:T(8,128)(2,1)}, bf16[576,96]{1,0:T(8,128)(2,1)S(1)}, u32[]{:S(2)}, u32[]{:S(2)}) collective-permute-start(bf16[576,96]{1,0:T(8,128)(2,1)} %pack_weights.1.own_ref), channel_id=1, source_target_pairs={{0,1},{1,0},{2,3},{3,2},{4,5},{5,4},{6,7},{7,6},{8,9},{9,8},{10,11... | collective-permute-start | bytes 331784 | tf_op jit(solution)/shard_map/ppermute | solution.py:622
  5.9 64.2 %frozen_block.1 = (bf16[2048,768]{1,0:T(8,128)(2,1)}, bf16[96,2048]{1,0:T(8,128)(2,1)}) custom-call(s32[4,1,1024]{2,1,0:T(1,128)} %bitcast.31, bf16[2048,768]{1,0:T(8,128)(2,1)} %x_ref.1, f32[768]{0:T(1024)} %before_ref.1, f32[768]{0:T(1024)} %middle_ref.1, bf16[96,768]{1,0:T(8,128)(2,1)} %bitcast.30, bf16[768,768]{1,0:T(8,128)(2,1)} %wq_hbm.1, ...), custom_call_target="tpu_custom_call" | custom-call | tf_op jit(solution)/shard_map/frozen_block/pallas_call | solution.py:208
  70.1 0.0 collective-permute-done.other_ref
  70.1 0.0 copy-start
  70.1 0.6 copy-done
  70.8 50.4 %side_block.1 = (bf16[96,2048]{1,0:T(8,128)(2,1)}, bf16[96,2048]{1,0:T(8,128)(2,1)}, bf16[4,192,128]{2,1,0:T(8,128)(2,1)}, bf16[4,192,128]{2,1,0:T(8,128)(2,1)}) custom-call(s32[1]{0:T(128)S(6)} %copy.35.index_ref, s32[4,1,1024]{2,1,0:T(1,128)} %bitcast.32, bf16[96,2048]{1,0:T(8,128)(2,1)} %get-tuple-element.28.tap_ref, bf16[96,2048]{1,0:T(8,128)(2,1)} %bitcast.28, ...), custom_call_target="tpu_custom_call" | custom-call | tf_op jit(solution)/shard_map/side_block/pallas_call | solution.py:517
  121.2 0.1 collective-permute-start.1
  121.2 1.6 %collective-permute-done.1 = bf16[4,192,128]{2,1,0:T(8,128)(2,1)S(1)} collective-permute-done((bf16[4,192,128]{2,1,0:T(8,128)(2,1)}, bf16[4,192,128]{2,1,0:T(8,128)(2,1)S(1)}, u32[]{:S(2)}, u32[]{:S(2)}) %collective-permute-start.1) | collective-permute-done | bytes 196640 | tf_op jit(solution)/shard_map/ppermute | solution.py:622
  122.9 1.0 add_convert_fusion
  123.9 0.1 collective-permute-start.2
  124.0 2.9 %collective-permute-start.4 = (bf16[192,128]{1,0:T(8,128)(2,1)S(1)}, bf16[192,128]{1,0:T(8,128)(2,1)S(1)}, u32[]{:S(2)}, u32[]{:S(2)}) collective-permute-start(bf16[192,128]{1,0:T(8,128)(2,1)S(1)} %get-tuple-element.45), channel_id=1, source_target_pairs={{0,5},{1,4},{2,7},{3,6},{4,1},{5,0},{6,3},{7,2},{8,13},{9,12},{10,... | collective-permute-start | bytes 147464 | tf_op jit(solution)/shard_map/ppermute | solution.py:622
  126.9 0.5 collective-permute-start.3
  127.4 1.7 %collective-permute-done.2 = bf16[192,128]{1,0:T(8,128)(2,1)S(1)} collective-permute-done((bf16[192,128]{1,0:T(8,128)(2,1)S(1)}, bf16[192,128]{1,0:T(8,128)(2,1)S(1)}, u32[]{:S(2)}, u32[]{:S(2)}) %collective-permute-start.2) | collective-permute-done | bytes 49184 | tf_op jit(solution)/shard_map/ppermute | solution.py:622
  129.1 0.0 collective-permute-done.4
  129.1 1.9 %collective-permute-done.3 = bf16[192,128]{1,0:T(8,128)(2,1)S(1)} collective-permute-done((bf16[192,128]{1,0:T(8,128)(2,1)S(1)}, bf16[192,128]{1,0:T(8,128)(2,1)S(1)}, u32[]{:S(2)}, u32[]{:S(2)}) %collective-permute-start.3) | collective-permute-done | bytes 49184 | tf_op jit(solution)/shard_map/ppermute | solution.py:622
  131.0 1.6 %collective-permute-start.5 = (bf16[192,128]{1,0:T(8,128)(2,1)S(1)}, bf16[192,128]{1,0:T(8,128)(2,1)S(1)}, u32[]{:S(2)}, u32[]{:S(2)}) collective-permute-start(bf16[192,128]{1,0:T(8,128)(2,1)S(1)} %fusion.2), channel_id=1, source_target_pairs={{0,8},{1,9},{2,10},{3,11},{4,12},{5,13},{6,14},{7,15},{8,0},{9,1},... | collective-permute-start | bytes 147464 | tf_op jit(solution)/shard_map/ppermute | solution.py:622
  132.7 2.5 %collective-permute-done.5 = bf16[192,128]{1,0:T(8,128)(2,1)S(1)} collective-permute-done((bf16[192,128]{1,0:T(8,128)(2,1)S(1)}, bf16[192,128]{1,0:T(8,128)(2,1)S(1)}, u32[]{:S(2)}, u32[]{:S(2)}) %collective-permute-start.5) | collective-permute-done | bytes 49184 | tf_op jit(solution)/shard_map/ppermute | solution.py:622
  135.2 2.7 %collective-permute-start.6 = (bf16[192,128]{1,0:T(8,128)(2,1)S(1)}, bf16[192,128]{1,0:T(8,128)(2,1)S(1)}, u32[]{:S(2)}, u32[]{:S(2)}) collective-permute-start(bf16[192,128]{1,0:T(8,128)(2,1)S(1)} %add_convert_fusion.2), channel_id=1, source_target_pairs={{0,16},{1,17},{2,18},{3,19},{4,20},{5,21},{6,22},{7,23},{8,24},{9,... | collective-permute-start | bytes 147464 | tf_op jit(solution)/shard_map/ppermute | solution.py:622
  137.8 2.4 %collective-permute-done.6 = bf16[192,128]{1,0:T(8,128)(2,1)S(1)} collective-permute-done((bf16[192,128]{1,0:T(8,128)(2,1)S(1)}, bf16[192,128]{1,0:T(8,128)(2,1)S(1)}, u32[]{:S(2)}, u32[]{:S(2)}) %collective-permute-start.6) | collective-permute-done | bytes 49184 | tf_op jit(solution)/shard_map/ppermute | solution.py:622
  140.3 0.6 collective-permute-start.7
  140.9 1.4 collective-permute-start.9
  142.3 1.5 %collective-permute-start.8 = (bf16[72,128]{1,0:T(8,128)(2,1)S(1)}, bf16[72,128]{1,0:T(8,128)(2,1)S(1)}, u32[]{:S(2)}, u32[]{:S(2)}) collective-permute-start(bf16[72,128]{1,0:T(8,128)(2,1)S(1)} %slice.25), channel_id=1, source_target_pairs={{0,1},{1,0},{2,3},{3,2},{4,5},{5,4},{6,7},{7,6},{8,9},{9,8},{10,11... | collective-permute-start | bytes 55304 | tf_op jit(solution)/shard_map/ppermute | solution.py:622
  143.8 1.7 %collective-permute-done.9 = bf16[72,128]{1,0:T(8,128)(2,1)S(1)} collective-permute-done((bf16[72,128]{1,0:T(8,128)(2,1)S(1)}, bf16[72,128]{1,0:T(8,128)(2,1)S(1)}, u32[]{:S(2)}, u32[]{:S(2)}) %collective-permute-start.9) | collective-permute-done | bytes 18464 | tf_op jit(solution)/shard_map/ppermute | solution.py:622
  145.5 0.5 collective-permute-done.8
  146.1 0.0 collective-permute-done.7
  146.1 0.1 collective-permute-start.10
  146.2 1.3 collective-permute-done.10.far_ref
  147.5 0.9 unpack_gradients.1
  (6 shorter events, 0.1 us)
Async XLA Ops:
  2.3 67.8 %collective-permute-start = (bf16[576,96]{1,0:T(8,128)(2,1)}, bf16[576,96]{1,0:T(8,128)(2,1)S(1)}, u32[]{:S(2)}, u32[]{:S(2)}) collective-permute-start(bf16[576,96]{1,0:T(8,128)(2,1)} %pack_weights.1.own_ref), channel_id=1, source_target_pairs={{0,1},{1,0},{2,3},{3,2},{4,5},{5,4},{6,7},{7,6},{8,9},{9,8},{10,11... | collective-permute-start | bytes 331784 | tf_op jit(solution)/shard_map/ppermute | solution.py:622
  70.1 0.7 copy-start
  121.2 1.7 %collective-permute-start.1 = (bf16[4,192,128]{2,1,0:T(8,128)(2,1)}, bf16[4,192,128]{2,1,0:T(8,128)(2,1)S(1)}, u32[]{:S(2)}, u32[]{:S(2)}) collective-permute-start(bf16[4,192,128]{2,1,0:T(8,128)(2,1)} %get-tuple-element.33), channel_id=1, source_target_pairs={{0,2},{1,3},{2,0},{3,1},{4,6},{5,7},{6,4},{7,5},{8,10},{9,11},{10,... | collective-permute-start | bytes 589832 | tf_op jit(solution)/shard_map/ppermute | solution.py:622
  123.9 5.2 %collective-permute-start.2 = (bf16[192,128]{1,0:T(8,128)(2,1)S(1)}, bf16[192,128]{1,0:T(8,128)(2,1)S(1)}, u32[]{:S(2)}, u32[]{:S(2)}) collective-permute-start(bf16[192,128]{1,0:T(8,128)(2,1)S(1)} %get-tuple-element.44), channel_id=1, source_target_pairs={{0,1},{1,0},{2,3},{3,2},{4,5},{5,4},{6,7},{7,6},{8,9},{9,8},{10,11... | collective-permute-start | bytes 147464 | tf_op jit(solution)/shard_map/ppermute | solution.py:622
  124.0 5.1 %collective-permute-start.4 = (bf16[192,128]{1,0:T(8,128)(2,1)S(1)}, bf16[192,128]{1,0:T(8,128)(2,1)S(1)}, u32[]{:S(2)}, u32[]{:S(2)}) collective-permute-start(bf16[192,128]{1,0:T(8,128)(2,1)S(1)} %get-tuple-element.45), channel_id=1, source_target_pairs={{0,5},{1,4},{2,7},{3,6},{4,1},{5,0},{6,3},{7,2},{8,13},{9,12},{10,... | collective-permute-start | bytes 147464 | tf_op jit(solution)/shard_map/ppermute | solution.py:622
  126.9 4.1 %collective-permute-start.3 = (bf16[192,128]{1,0:T(8,128)(2,1)S(1)}, bf16[192,128]{1,0:T(8,128)(2,1)S(1)}, u32[]{:S(2)}, u32[]{:S(2)}) collective-permute-start(bf16[192,128]{1,0:T(8,128)(2,1)S(1)} %get-tuple-element.46), channel_id=1, source_target_pairs={{0,4},{1,5},{2,6},{3,7},{4,0},{5,1},{6,2},{7,3},{8,12},{9,13},{10,... | collective-permute-start | bytes 147464 | tf_op jit(solution)/shard_map/ppermute | solution.py:622
  131.0 4.2 %collective-permute-start.5 = (bf16[192,128]{1,0:T(8,128)(2,1)S(1)}, bf16[192,128]{1,0:T(8,128)(2,1)S(1)}, u32[]{:S(2)}, u32[]{:S(2)}) collective-permute-start(bf16[192,128]{1,0:T(8,128)(2,1)S(1)} %fusion.2), channel_id=1, source_target_pairs={{0,8},{1,9},{2,10},{3,11},{4,12},{5,13},{6,14},{7,15},{8,0},{9,1},... | collective-permute-start | bytes 147464 | tf_op jit(solution)/shard_map/ppermute | solution.py:622
  135.2 5.1 %collective-permute-start.6 = (bf16[192,128]{1,0:T(8,128)(2,1)S(1)}, bf16[192,128]{1,0:T(8,128)(2,1)S(1)}, u32[]{:S(2)}, u32[]{:S(2)}) collective-permute-start(bf16[192,128]{1,0:T(8,128)(2,1)S(1)} %add_convert_fusion.2), channel_id=1, source_target_pairs={{0,16},{1,17},{2,18},{3,19},{4,20},{5,21},{6,22},{7,23},{8,24},{9,... | collective-permute-start | bytes 147464 | tf_op jit(solution)/shard_map/ppermute | solution.py:622
  140.3 5.8 %collective-permute-start.7 = (bf16[192,128]{1,0:T(8,128)(2,1)S(1)}, bf16[192,128]{1,0:T(8,128)(2,1)S(1)}, u32[]{:S(2)}, u32[]{:S(2)}) collective-permute-start(bf16[192,128]{1,0:T(8,128)(2,1)S(1)} %add_convert_fusion.1), channel_id=1, source_target_pairs={{0,4},{1,5},{2,6},{3,7},{4,0},{5,1},{6,2},{7,3},{8,12},{9,13},{10,... | collective-permute-start | bytes 147464 | tf_op jit(solution)/shard_map/ppermute | solution.py:622
  140.9 4.7 %collective-permute-start.9 = (bf16[72,128]{1,0:T(8,128)(2,1)S(1)}, bf16[72,128]{1,0:T(8,128)(2,1)S(1)}, u32[]{:S(2)}, u32[]{:S(2)}) collective-permute-start(bf16[72,128]{1,0:T(8,128)(2,1)S(1)} %slice.25), channel_id=1, source_target_pairs={{0,5},{1,4},{2,7},{3,6},{4,1},{5,0},{6,3},{7,2},{8,13},{9,12},{10,... | collective-permute-start | bytes 55304 | tf_op jit(solution)/shard_map/ppermute | solution.py:622
  142.3 3.8 %collective-permute-start.8 = (bf16[72,128]{1,0:T(8,128)(2,1)S(1)}, bf16[72,128]{1,0:T(8,128)(2,1)S(1)}, u32[]{:S(2)}, u32[]{:S(2)}) collective-permute-start(bf16[72,128]{1,0:T(8,128)(2,1)S(1)} %slice.25), channel_id=1, source_target_pairs={{0,1},{1,0},{2,3},{3,2},{4,5},{5,4},{6,7},{7,6},{8,9},{9,8},{10,11... | collective-permute-start | bytes 55304 | tf_op jit(solution)/shard_map/ppermute | solution.py:622
  146.1 1.4 collective-permute-start.10

commit v2 on v1

--- a/solution.py
+++ b/solution.py
@@ -15,7 +15,7 @@
 LOG2E = 1.4426950408889634
 LEAST = 2.0**-64
 MOST = 2.0**64
-TILE = 512
+TILE = 1024
 ROWS = 96
 GROUP = 4
 PAIRS = 2
@@ -344,7 +344,7 @@
     zeros8 = jnp.zeros((SIDE_HEAD, SEQ), F32)
     ones8 = jnp.ones((SIDE_HEAD, SEQ), F32)
 
-    def prepare(head, carry):
+    def prepare(head):
         q = qkv_ref[head_rows(0, head)] * (SIDE_HEAD**-0.5 * LOG2E)
         q = q.astype(BF16).astype(F32)
         k = qkv_ref[head_rows(1, head)].astype(BF16).astype(F32)
@@ -356,9 +356,13 @@
         k16_ref[head] = jnp.concatenate([k, zeros8], axis=0).astype(BF16)
         rows = [v, ones8, k, zeros8] + outer_rows(v, k)
         rows_ref[head] = jnp.concatenate(rows, axis=0).astype(BF16)
+
+    def prepare_group(group, carry):
+        for turn in range(GROUP):
+            prepare(group * GROUP + turn)
         return carry
 
-    lax.fori_loop(0, heads, prepare, 0)
+    lax.fori_loop(0, heads // GROUP, prepare_group, 0)
 
     def attend(careful, tile):
         def one(head, start):
@@ -417,7 +421,7 @@
     out_grad_ref[...] += dot(low_dres, ctx, NT)
     dctx_ref[...] = dot(wo_ref[...], low_dres).astype(BF16).astype(F32)
 
-    def prepare_back(head, carry):
+    def prepare_back(head):
         at = pl.multiple_of(head * SIDE_HEAD, SIDE_HEAD)
         q = qkv_ref[head_rows(0, head)]
         dctx = dctx_ref[pl.ds(at, SIDE_HEAD)]
@@ -431,9 +435,13 @@
         scaled = dctx * inverse
         rows = [scaled, zeros8, (inner * inverse) * q, zeros8] + outer_rows(scaled, q)
         rows_ref[head] = jnp.concatenate(rows, axis=0).astype(BF16)
+
+    def prepare_back_group(group, carry):
+        for turn in range(GROUP):
+            prepare_back(group * GROUP + turn)
         return carry
 
-    lax.fori_loop(0, heads, prepare_back, 0)
+    lax.fori_loop(0, heads // GROUP, prepare_back_group, 0)
 
     def back(head):
         found = dot(rows_ref[head], e_ref[head])
@@ -696,8 +704,9 @@
     mine = add(quad[0], swap(quad[1], 0, 1), swap(quad[2], 2, 0), swap(quad[3], 2, 1))
     bit = 4
     while bit < dp_size:
-        mine = add(mine, swap(mine, bit, 0))
-        bit *= 2
+        steps = [bit, 2 * bit, 3 * bit] if 2 * bit < dp_size else [bit]
+        mine = add(mine, *[swap(mine, step, 0) for step in steps])
+        bit *= len(steps) + 1
     near = jnp.concatenate(
         [mine, swap(mine, 2, 0), swap(mine[:taps], 0, 1), swap(mine[:taps], 2, 1)], axis=0
     )

time: 149 us -> 147 us (0.987)
    ppermute x11 -> x12, waiting for transfers between devices: 13.7 us -> 13 us  [exchange(): return lax.ppermute(values, ('dp', 'side'), pairs)]
    ppermute x11 -> x12, starting transfers between devices: 14.5 us -> 14.7 us  [exchange(): return lax.ppermute(values, ('dp', 'side'), pairs)]
  transfers between devices with their start and end apart: 11 -> 12, of which waited for: 8 -> 8; matrix products, arithmetic and copies ran while one was open for 0% -> 0% of each run, Pallas kernels for 43% -> 44%
where the time goes in v2:
time: 147 us
  Pallas kernels  116 us (79%)
  starting transfers between devices  14.7 us (10%)
  waiting for transfers between devices  13 us (9%)
    pallas_call x1, Pallas kernels, frozen_block(): pl.pallas_call(frozen_kernel, grid=(tokens // SEQ,), in_specs=[whole(segm...  64.6 us
    pallas_call x1, Pallas kernels, side_block(): pl.pallas_call(side_kernel, grid=(tokens // SEQ,), in_specs=[pl.BlockSpec...  49.1 us
    ppermute x12, starting transfers between devices, exchange(): return lax.ppermute(values, ('dp', 'side'), pairs)  14.7 us
    ppermute x12, waiting for transfers between devices, exchange(): return lax.ppermute(values, ('dp', 'side'), pairs)  13 us
  transfers between devices with their start and end apart: 12, of which 8 were waited for; matrix products, arithmetic and copies ran while one was open for 0% of the time, Pallas kernels for 44%

profile of v2, /device:TPU:0, one launch (start us, length us, event | category | flops | bytes accessed | tf_op | source)
XLA Modules:
  0.0 147.1 jit_solution(12076723047728837573)
XLA Ops:
  0.6 1.6 %pack_weights.1.own_ref = bf16[576,96]{1,0:T(8,128)(2,1)} custom-call(bf16[96,192]{1,0:T(8,128)(2,1)} %expand_ref.1, bf16[48,96]{1,0:T(8,128)(2,1)} %bitcast.33, bf16[48,96]{1,0:T(8,128)(2,1)} %bitcast.34, bf16[48,96]{1,0:T(8,128)(2,1)} %bitcast.35, bf16[48,96]{1,0:T(8,128)(2,1)} %output_ref.1, bf16[192,96]{1,0:T(8,128)(2,1)} %reduce_ref.1), custom_call_target="tpu_custom_call" | custom-call | tf_op jit(solution)/shard_map/pack_weights/pallas_call | solution.py:668
  2.3 3.0 %collective-permute-start = (bf16[576,96]{1,0:T(8,128)(2,1)}, bf16[576,96]{1,0:T(8,128)(2,1)S(1)}, u32[]{:S(2)}, u32[]{:S(2)}) collective-permute-start(bf16[576,96]{1,0:T(8,128)(2,1)} %pack_weights.1.own_ref), channel_id=1, source_target_pairs={{0,1},{1,0},{2,3},{3,2},{4,5},{5,4},{6,7},{7,6},{8,9},{9,8},{10,11... | collective-permute-start | bytes 331784 | tf_op jit(solution)/shard_map/ppermute | solution.py:630
  5.9 64.6 %frozen_block.1 = (bf16[2048,768]{1,0:T(8,128)(2,1)}, bf16[96,2048]{1,0:T(8,128)(2,1)}) custom-call(s32[4,1,1024]{2,1,0:T(1,128)} %bitcast.31, bf16[2048,768]{1,0:T(8,128)(2,1)} %x_ref.1, f32[768]{0:T(1024)} %before_ref.1, f32[768]{0:T(1024)} %middle_ref.1, bf16[96,768]{1,0:T(8,128)(2,1)} %bitcast.30, bf16[768,768]{1,0:T(8,128)(2,1)} %wq_hbm.1, ...), custom_call_target="tpu_custom_call" | custom-call | tf_op jit(solution)/shard_map/frozen_block/pallas_call | solution.py:208
  70.6 0.0 collective-permute-done.other_ref
  70.6 0.0 copy-start
  70.6 0.6 copy-done
  71.2 49.1 %side_block.1 = (bf16[96,2048]{1,0:T(8,128)(2,1)}, bf16[96,2048]{1,0:T(8,128)(2,1)}, bf16[4,192,128]{2,1,0:T(8,128)(2,1)}, bf16[4,192,128]{2,1,0:T(8,128)(2,1)}) custom-call(s32[1]{0:T(128)S(6)} %copy.35.index_ref, s32[4,1,1024]{2,1,0:T(1,128)} %bitcast.32, bf16[96,2048]{1,0:T(8,128)(2,1)} %get-tuple-element.28.tap_ref, bf16[96,2048]{1,0:T(8,128)(2,1)} %bitcast.28, ...), custom_call_target="tpu_custom_call" | custom-call | tf_op jit(solution)/shard_map/side_block/pallas_call | solution.py:525
  120.4 0.1 collective-permute-start.1
  120.4 1.6 %collective-permute-done.1 = bf16[4,192,128]{2,1,0:T(8,128)(2,1)S(1)} collective-permute-done((bf16[4,192,128]{2,1,0:T(8,128)(2,1)}, bf16[4,192,128]{2,1,0:T(8,128)(2,1)S(1)}, u32[]{:S(2)}, u32[]{:S(2)}) %collective-permute-start.1) | collective-permute-done | bytes 196640 | tf_op jit(solution)/shard_map/ppermute | solution.py:630
  122.1 1.0 add_convert_fusion
  123.1 0.1 collective-permute-start.2
  123.2 2.9 %collective-permute-start.4 = (bf16[192,128]{1,0:T(8,128)(2,1)S(1)}, bf16[192,128]{1,0:T(8,128)(2,1)S(1)}, u32[]{:S(2)}, u32[]{:S(2)}) collective-permute-start(bf16[192,128]{1,0:T(8,128)(2,1)S(1)} %get-tuple-element.45), channel_id=1, source_target_pairs={{0,5},{1,4},{2,7},{3,6},{4,1},{5,0},{6,3},{7,2},{8,13},{9,12},{10,... | collective-permute-start | bytes 147464 | tf_op jit(solution)/shard_map/ppermute | solution.py:630
  126.1 0.5 collective-permute-start.3
  126.6 1.7 %collective-permute-done.2 = bf16[192,128]{1,0:T(8,128)(2,1)S(1)} collective-permute-done((bf16[192,128]{1,0:T(8,128)(2,1)S(1)}, bf16[192,128]{1,0:T(8,128)(2,1)S(1)}, u32[]{:S(2)}, u32[]{:S(2)}) %collective-permute-start.2) | collective-permute-done | bytes 49184 | tf_op jit(solution)/shard_map/ppermute | solution.py:630
  128.3 0.0 collective-permute-done.4
  128.3 1.9 %collective-permute-done.3 = bf16[192,128]{1,0:T(8,128)(2,1)S(1)} collective-permute-done((bf16[192,128]{1,0:T(8,128)(2,1)S(1)}, bf16[192,128]{1,0:T(8,128)(2,1)S(1)}, u32[]{:S(2)}, u32[]{:S(2)}) %collective-permute-start.3) | collective-permute-done | bytes 49184 | tf_op jit(solution)/shard_map/ppermute | solution.py:630
  130.2 3.7 %collective-permute-start.7 = (bf16[192,128]{1,0:T(8,128)(2,1)S(1)}, bf16[192,128]{1,0:T(8,128)(2,1)S(1)}, u32[]{:S(2)}, u32[]{:S(2)}) collective-permute-start(bf16[192,128]{1,0:T(8,128)(2,1)S(1)} %fusion.2), channel_id=1, source_target_pairs={{0,24},{1,25},{2,26},{3,27},{4,28},{5,29},{6,30},{7,31},{8,16},{9,... | collective-permute-start | bytes 147464 | tf_op jit(solution)/shard_map/ppermute | solution.py:630
  133.9 0.0 collective-permute-start.6
  133.9 0.8 collective-permute-start.5
  134.7 1.6 %collective-permute-done.7 = bf16[192,128]{1,0:T(8,128)(2,1)S(1)} collective-permute-done((bf16[192,128]{1,0:T(8,128)(2,1)S(1)}, bf16[192,128]{1,0:T(8,128)(2,1)S(1)}, u32[]{:S(2)}, u32[]{:S(2)}) %collective-permute-start.7) | collective-permute-done | bytes 49184 | tf_op jit(solution)/shard_map/ppermute | solution.py:630
  136.3 2.6 %collective-permute-done.6 = bf16[192,128]{1,0:T(8,128)(2,1)S(1)} collective-permute-done((bf16[192,128]{1,0:T(8,128)(2,1)S(1)}, bf16[192,128]{1,0:T(8,128)(2,1)S(1)}, u32[]{:S(2)}, u32[]{:S(2)}) %collective-permute-start.6) | collective-permute-done | bytes 49184 | tf_op jit(solution)/shard_map/ppermute | solution.py:630
  138.9 0.0 collective-permute-done.5
  138.9 0.6 collective-permute-start.8
  139.5 1.4 collective-permute-start.10
  141.0 1.5 %collective-permute-start.9 = (bf16[72,128]{1,0:T(8,128)(2,1)S(1)}, bf16[72,128]{1,0:T(8,128)(2,1)S(1)}, u32[]{:S(2)}, u32[]{:S(2)}) collective-permute-start(bf16[72,128]{1,0:T(8,128)(2,1)S(1)} %slice.25), channel_id=1, source_target_pairs={{0,1},{1,0},{2,3},{3,2},{4,5},{5,4},{6,7},{7,6},{8,9},{9,8},{10,11... | collective-permute-start | bytes 55304 | tf_op jit(solution)/shard_map/ppermute | solution.py:630
  142.5 1.7 %collective-permute-done.10 = bf16[72,128]{1,0:T(8,128)(2,1)S(1)} collective-permute-done((bf16[72,128]{1,0:T(8,128)(2,1)S(1)}, bf16[72,128]{1,0:T(8,128)(2,1)S(1)}, u32[]{:S(2)}, u32[]{:S(2)}) %collective-permute-start.10) | collective-permute-done | bytes 18464 | tf_op jit(solution)/shard_map/ppermute | solution.py:630
  144.2 0.5 collective-permute-done.9
  144.7 0.0 collective-permute-done.8
  144.7 0.1 collective-permute-start.11
  144.8 1.3 collective-permute-done.11.far_ref
  146.2 0.9 unpack_gradients.1
  (5 shorter events, 0.1 us)
Async XLA Ops:
  2.3 68.3 %collective-permute-start = (bf16[576,96]{1,0:T(8,128)(2,1)}, bf16[576,96]{1,0:T(8,128)(2,1)S(1)}, u32[]{:S(2)}, u32[]{:S(2)}) collective-permute-start(bf16[576,96]{1,0:T(8,128)(2,1)} %pack_weights.1.own_ref), channel_id=1, source_target_pairs={{0,1},{1,0},{2,3},{3,2},{4,5},{5,4},{6,7},{7,6},{8,9},{9,8},{10,11... | collective-permute-start | bytes 331784 | tf_op jit(solution)/shard_map/ppermute | solution.py:630
  70.6 0.7 copy-start
  120.4 1.7 %collective-permute-start.1 = (bf16[4,192,128]{2,1,0:T(8,128)(2,1)}, bf16[4,192,128]{2,1,0:T(8,128)(2,1)S(1)}, u32[]{:S(2)}, u32[]{:S(2)}) collective-permute-start(bf16[4,192,128]{2,1,0:T(8,128)(2,1)} %get-tuple-element.33), channel_id=1, source_target_pairs={{0,2},{1,3},{2,0},{3,1},{4,6},{5,7},{6,4},{7,5},{8,10},{9,11},{10,... | collective-permute-start | bytes 589832 | tf_op jit(solution)/shard_map/ppermute | solution.py:630
  123.1 5.2 %collective-permute-start.2 = (bf16[192,128]{1,0:T(8,128)(2,1)S(1)}, bf16[192,128]{1,0:T(8,128)(2,1)S(1)}, u32[]{:S(2)}, u32[]{:S(2)}) collective-permute-start(bf16[192,128]{1,0:T(8,128)(2,1)S(1)} %get-tuple-element.44), channel_id=1, source_target_pairs={{0,1},{1,0},{2,3},{3,2},{4,5},{5,4},{6,7},{7,6},{8,9},{9,8},{10,11... | collective-permute-start | bytes 147464 | tf_op jit(solution)/shard_map/ppermute | solution.py:630
  123.2 5.1 %collective-permute-start.4 = (bf16[192,128]{1,0:T(8,128)(2,1)S(1)}, bf16[192,128]{1,0:T(8,128)(2,1)S(1)}, u32[]{:S(2)}, u32[]{:S(2)}) collective-permute-start(bf16[192,128]{1,0:T(8,128)(2,1)S(1)} %get-tuple-element.45), channel_id=1, source_target_pairs={{0,5},{1,4},{2,7},{3,6},{4,1},{5,0},{6,3},{7,2},{8,13},{9,12},{10,... | collective-permute-start | bytes 147464 | tf_op jit(solution)/shard_map/ppermute | solution.py:630
  126.1 4.1 %collective-permute-start.3 = (bf16[192,128]{1,0:T(8,128)(2,1)S(1)}, bf16[192,128]{1,0:T(8,128)(2,1)S(1)}, u32[]{:S(2)}, u32[]{:S(2)}) collective-permute-start(bf16[192,128]{1,0:T(8,128)(2,1)S(1)} %get-tuple-element.46), channel_id=1, source_target_pairs={{0,4},{1,5},{2,6},{3,7},{4,0},{5,1},{6,2},{7,3},{8,12},{9,13},{10,... | collective-permute-start | bytes 147464 | tf_op jit(solution)/shard_map/ppermute | solution.py:630
  130.2 6.0 %collective-permute-start.7 = (bf16[192,128]{1,0:T(8,128)(2,1)S(1)}, bf16[192,128]{1,0:T(8,128)(2,1)S(1)}, u32[]{:S(2)}, u32[]{:S(2)}) collective-permute-start(bf16[192,128]{1,0:T(8,128)(2,1)S(1)} %fusion.2), channel_id=1, source_target_pairs={{0,24},{1,25},{2,26},{3,27},{4,28},{5,29},{6,30},{7,31},{8,16},{9,... | collective-permute-start | bytes 147464 | tf_op jit(solution)/shard_map/ppermute | solution.py:630
  133.9 5.0 %collective-permute-start.6 = (bf16[192,128]{1,0:T(8,128)(2,1)S(1)}, bf16[192,128]{1,0:T(8,128)(2,1)S(1)}, u32[]{:S(2)}, u32[]{:S(2)}) collective-permute-start(bf16[192,128]{1,0:T(8,128)(2,1)S(1)} %fusion.2), channel_id=1, source_target_pairs={{0,16},{1,17},{2,18},{3,19},{4,20},{5,21},{6,22},{7,23},{8,24},{9,... | collective-permute-start | bytes 147464 | tf_op jit(solution)/shard_map/ppermute | solution.py:630
  133.9 5.0 %collective-permute-start.5 = (bf16[192,128]{1,0:T(8,128)(2,1)S(1)}, bf16[192,128]{1,0:T(8,128)(2,1)S(1)}, u32[]{:S(2)}, u32[]{:S(2)}) collective-permute-start(bf16[192,128]{1,0:T(8,128)(2,1)S(1)} %fusion.2), channel_id=1, source_target_pairs={{0,8},{1,9},{2,10},{3,11},{4,12},{5,13},{6,14},{7,15},{8,0},{9,1},... | collective-permute-start | bytes 147464 | tf_op jit(solution)/shard_map/ppermute | solution.py:630
  138.9 5.8 %collective-permute-start.8 = (bf16[192,128]{1,0:T(8,128)(2,1)S(1)}, bf16[192,128]{1,0:T(8,128)(2,1)S(1)}, u32[]{:S(2)}, u32[]{:S(2)}) collective-permute-start(bf16[192,128]{1,0:T(8,128)(2,1)S(1)} %add_convert_fusion.1), channel_id=1, source_target_pairs={{0,4},{1,5},{2,6},{3,7},{4,0},{5,1},{6,2},{7,3},{8,12},{9,13},{10,... | collective-permute-start | bytes 147464 | tf_op jit(solution)/shard_map/ppermute | solution.py:630
  139.5 4.7 %collective-permute-start.10 = (bf16[72,128]{1,0:T(8,128)(2,1)S(1)}, bf16[72,128]{1,0:T(8,128)(2,1)S(1)}, u32[]{:S(2)}, u32[]{:S(2)}) collective-permute-start(bf16[72,128]{1,0:T(8,128)(2,1)S(1)} %slice.25), channel_id=1, source_target_pairs={{0,5},{1,4},{2,7},{3,6},{4,1},{5,0},{6,3},{7,2},{8,13},{9,12},{10,... | collective-permute-start | bytes 55304 | tf_op jit(solution)/shard_map/ppermute | solution.py:630
  141.0 3.8 %collective-permute-start.9 = (bf16[72,128]{1,0:T(8,128)(2,1)S(1)}, bf16[72,128]{1,0:T(8,128)(2,1)S(1)}, u32[]{:S(2)}, u32[]{:S(2)}) collective-permute-start(bf16[72,128]{1,0:T(8,128)(2,1)S(1)} %slice.25), channel_id=1, source_target_pairs={{0,1},{1,0},{2,3},{3,2},{4,5},{5,4},{6,7},{7,6},{8,9},{9,8},{10,11... | collective-permute-start | bytes 55304 | tf_op jit(solution)/shard_map/ppermute | solution.py:630
  144.7 1.4 collective-permute-start.11

commit v3 on v2

--- a/solution.py
+++ b/solution.py
@@ -18,7 +18,7 @@
 TILE = 1024
 ROWS = 96
 GROUP = 4
-PAIRS = 2
+PAIRS = 3
 
 F32 = jnp.float32
 BF16 = jnp.bfloat16
@@ -124,11 +124,6 @@
             copy.start()
         v_ref[:, HEAD:padded] = jnp.ones((heads, padded - HEAD, SEQ), BF16)
 
-    here = lax.axis_index("side") * pl.num_programs(0) + pl.program_id(0)
-    fill_mask(segment_ref[here], mask_ref)
-    base = x_ref[...].astype(F32)
-    factor = lax.rsqrt(jnp.mean(base * base, axis=-1, keepdims=True) + EPS)
-    normed_ref[...] = (base * factor * before_ref[...][None]).astype(BF16)
     @pl.when(starting)
     def _():
         for copy in copies[0:3]:
@@ -137,8 +132,16 @@
             copy.start()
         wv_t_ref[...] = jnp.transpose(wv_ref[...])
 
-    q_ref[...] = (dot(normed_ref[...], wq_ref[...]) * (HEAD**-0.5 * LOG2E)).astype(BF16)
-    k_ref[...] = dot(normed_ref[...], wk_ref[...]).astype(BF16)
+    for part in range(2):
+        rows = slice(part * SEQ // 2, (part + 1) * SEQ // 2)
+        base = x_ref[rows].astype(F32)
+        factor = lax.rsqrt(jnp.mean(base * base, axis=-1, keepdims=True) + EPS)
+        normed = (base * factor * before_ref[...][None]).astype(BF16)
+        normed_ref[rows] = normed
+        q_ref[rows] = (dot(normed, wq_ref[...]) * (HEAD**-0.5 * LOG2E)).astype(BF16)
+        k_ref[rows] = dot(normed, wk_ref[...]).astype(BF16)
+    here = lax.axis_index("side") * pl.num_programs(0) + pl.program_id(0)
+    fill_mask(segment_ref[here], mask_ref)
     v = dot(wv_t_ref[...], normed_ref[...], NT).astype(BF16)
     for head in range(heads):
         v_ref[head, 0:HEAD] = v[head * HEAD : (head + 1) * HEAD]
@@ -316,8 +319,6 @@
         reduce_grad_ref[...] = jnp.zeros_like(reduce_grad_ref)
         small_ref[...] = jnp.zeros_like(small_ref)
 
-    here = lax.axis_index("side") * pl.num_programs(0) + pl.program_id(0)
-    fill_mask(segment_ref[here], mask_ref)
     logits = table_ref[pl.ds(index_ref[0], 1), :]
     stacked = jnp.concatenate(
         [
@@ -340,6 +341,9 @@
     factor1 = lax.rsqrt(jnp.mean(mixed * mixed, axis=0, keepdims=True) + EPS)
     n1 = (mixed * factor1 * before).astype(BF16)
     qkv_ref[...] = dot(w_ref[...], n1)
+
+    here = lax.axis_index("side") * pl.num_programs(0) + pl.program_id(0)
+    fill_mask(segment_ref[here], mask_ref)
 
     zeros8 = jnp.zeros((SIDE_HEAD, SEQ), F32)
     ones8 = jnp.ones((SIDE_HEAD, SEQ), F32)

time: 147 us -> 146 us (level)
  no operation moved by 1% of the time
where the time goes in v3:
time: 146 us
  Pallas kernels  115 us (79%)
  starting transfers between devices  14.7 us (10%)
  waiting for transfers between devices  13 us (9%)
    pallas_call x1, Pallas kernels, frozen_block(): pl.pallas_call(frozen_kernel, grid=(tokens // SEQ,), in_specs=[whole(segm...  63.4 us
    pallas_call x1, Pallas kernels, side_block(): pl.pallas_call(side_kernel, grid=(tokens // SEQ,), in_specs=[pl.BlockSpec...  49 us
    ppermute x12, starting transfers between devices, exchange(): return lax.ppermute(values, ('dp', 'side'), pairs)  14.7 us
    ppermute x12, waiting for transfers between devices, exchange(): return lax.ppermute(values, ('dp', 'side'), pairs)  13 us
  transfers between devices with their start and end apart: 12, of which 8 were waited for; matrix products, arithmetic and copies ran while one was open for 0% of the time, Pallas kernels for 44%

profile of v3, /device:TPU:0, one launch (start us, length us, event | category | flops | bytes accessed | tf_op | source)
XLA Modules:
  0.0 145.6 jit_solution(4963444633744851561)
XLA Ops:
  0.6 1.6 %pack_weights.1.own_ref = bf16[576,96]{1,0:T(8,128)(2,1)} custom-call(bf16[96,192]{1,0:T(8,128)(2,1)} %expand_ref.1, bf16[48,96]{1,0:T(8,128)(2,1)} %bitcast.33, bf16[48,96]{1,0:T(8,128)(2,1)} %bitcast.34, bf16[48,96]{1,0:T(8,128)(2,1)} %bitcast.35, bf16[48,96]{1,0:T(8,128)(2,1)} %output_ref.1, bf16[192,96]{1,0:T(8,128)(2,1)} %reduce_ref.1), custom_call_target="tpu_custom_call" | custom-call | tf_op jit(solution)/shard_map/pack_weights/pallas_call | solution.py:672
  2.3 3.0 %collective-permute-start = (bf16[576,96]{1,0:T(8,128)(2,1)}, bf16[576,96]{1,0:T(8,128)(2,1)S(1)}, u32[]{:S(2)}, u32[]{:S(2)}) collective-permute-start(bf16[576,96]{1,0:T(8,128)(2,1)} %pack_weights.1.own_ref), channel_id=1, source_target_pairs={{0,1},{1,0},{2,3},{3,2},{4,5},{5,4},{6,7},{7,6},{8,9},{9,8},{10,11... | collective-permute-start | bytes 331784 | tf_op jit(solution)/shard_map/ppermute | solution.py:634
  5.9 63.4 %frozen_block.1 = (bf16[2048,768]{1,0:T(8,128)(2,1)}, bf16[96,2048]{1,0:T(8,128)(2,1)}) custom-call(s32[4,1,1024]{2,1,0:T(1,128)} %bitcast.31, bf16[2048,768]{1,0:T(8,128)(2,1)} %x_ref.1, f32[768]{0:T(1024)} %before_ref.1, f32[768]{0:T(1024)} %middle_ref.1, bf16[96,768]{1,0:T(8,128)(2,1)} %bitcast.30, bf16[768,768]{1,0:T(8,128)(2,1)} %wq_hbm.1, ...), custom_call_target="tpu_custom_call" | custom-call | tf_op jit(solution)/shard_map/frozen_block/pallas_call | solution.py:211
  69.3 0.0 collective-permute-done.other_ref
  69.3 0.0 copy-start
  69.3 0.6 copy-done
  69.9 49.0 %side_block.1 = (bf16[96,2048]{1,0:T(8,128)(2,1)}, bf16[96,2048]{1,0:T(8,128)(2,1)}, bf16[4,192,128]{2,1,0:T(8,128)(2,1)}, bf16[4,192,128]{2,1,0:T(8,128)(2,1)}) custom-call(s32[1]{0:T(128)S(6)} %copy.35.index_ref, s32[4,1,1024]{2,1,0:T(1,128)} %bitcast.32, bf16[96,2048]{1,0:T(8,128)(2,1)} %get-tuple-element.28.tap_ref, bf16[96,2048]{1,0:T(8,128)(2,1)} %bitcast.28, ...), custom_call_target="tpu_custom_call" | custom-call | tf_op jit(solution)/shard_map/side_block/pallas_call | solution.py:529
  118.9 0.1 collective-permute-start.1
  119.0 1.6 %collective-permute-done.1 = bf16[4,192,128]{2,1,0:T(8,128)(2,1)S(1)} collective-permute-done((bf16[4,192,128]{2,1,0:T(8,128)(2,1)}, bf16[4,192,128]{2,1,0:T(8,128)(2,1)S(1)}, u32[]{:S(2)}, u32[]{:S(2)}) %collective-permute-start.1) | collective-permute-done | bytes 196640 | tf_op jit(solution)/shard_map/ppermute | solution.py:634
  120.6 1.0 add_convert_fusion
  121.6 0.1 collective-permute-start.2
  121.7 2.9 %collective-permute-start.4 = (bf16[192,128]{1,0:T(8,128)(2,1)S(1)}, bf16[192,128]{1,0:T(8,128)(2,1)S(1)}, u32[]{:S(2)}, u32[]{:S(2)}) collective-permute-start(bf16[192,128]{1,0:T(8,128)(2,1)S(1)} %get-tuple-element.45), channel_id=1, source_target_pairs={{0,5},{1,4},{2,7},{3,6},{4,1},{5,0},{6,3},{7,2},{8,13},{9,12},{10,... | collective-permute-start | bytes 147464 | tf_op jit(solution)/shard_map/ppermute | solution.py:634
  124.7 0.5 collective-permute-start.3
  125.2 1.7 %collective-permute-done.2 = bf16[192,128]{1,0:T(8,128)(2,1)S(1)} collective-permute-done((bf16[192,128]{1,0:T(8,128)(2,1)S(1)}, bf16[192,128]{1,0:T(8,128)(2,1)S(1)}, u32[]{:S(2)}, u32[]{:S(2)}) %collective-permute-start.2) | collective-permute-done | bytes 49184 | tf_op jit(solution)/shard_map/ppermute | solution.py:634
  126.8 0.0 collective-permute-done.4
  126.8 1.9 %collective-permute-done.3 = bf16[192,128]{1,0:T(8,128)(2,1)S(1)} collective-permute-done((bf16[192,128]{1,0:T(8,128)(2,1)S(1)}, bf16[192,128]{1,0:T(8,128)(2,1)S(1)}, u32[]{:S(2)}, u32[]{:S(2)}) %collective-permute-start.3) | collective-permute-done | bytes 49184 | tf_op jit(solution)/shard_map/ppermute | solution.py:634
  128.8 3.7 %collective-permute-start.7 = (bf16[192,128]{1,0:T(8,128)(2,1)S(1)}, bf16[192,128]{1,0:T(8,128)(2,1)S(1)}, u32[]{:S(2)}, u32[]{:S(2)}) collective-permute-start(bf16[192,128]{1,0:T(8,128)(2,1)S(1)} %fusion.2), channel_id=1, source_target_pairs={{0,24},{1,25},{2,26},{3,27},{4,28},{5,29},{6,30},{7,31},{8,16},{9,... | collective-permute-start | bytes 147464 | tf_op jit(solution)/shard_map/ppermute | solution.py:634
  132.4 0.0 collective-permute-start.6
  132.4 0.8 collective-permute-start.5
  133.2 1.6 %collective-permute-done.7 = bf16[192,128]{1,0:T(8,128)(2,1)S(1)} collective-permute-done((bf16[192,128]{1,0:T(8,128)(2,1)S(1)}, bf16[192,128]{1,0:T(8,128)(2,1)S(1)}, u32[]{:S(2)}, u32[]{:S(2)}) %collective-permute-start.7) | collective-permute-done | bytes 49184 | tf_op jit(solution)/shard_map/ppermute | solution.py:634
  134.8 2.6 %collective-permute-done.6 = bf16[192,128]{1,0:T(8,128)(2,1)S(1)} collective-permute-done((bf16[192,128]{1,0:T(8,128)(2,1)S(1)}, bf16[192,128]{1,0:T(8,128)(2,1)S(1)}, u32[]{:S(2)}, u32[]{:S(2)}) %collective-permute-start.6) | collective-permute-done | bytes 49184 | tf_op jit(solution)/shard_map/ppermute | solution.py:634
  137.4 0.0 collective-permute-done.5
  137.5 0.6 collective-permute-start.8
  138.1 1.5 %collective-permute-start.10 = (bf16[72,128]{1,0:T(8,128)(2,1)S(1)}, bf16[72,128]{1,0:T(8,128)(2,1)S(1)}, u32[]{:S(2)}, u32[]{:S(2)}) collective-permute-start(bf16[72,128]{1,0:T(8,128)(2,1)S(1)} %slice.25), channel_id=1, source_target_pairs={{0,5},{1,4},{2,7},{3,6},{4,1},{5,0},{6,3},{7,2},{8,13},{9,12},{10,... | collective-permute-start | bytes 55304 | tf_op jit(solution)/shard_map/ppermute | solution.py:634
  139.5 1.5 %collective-permute-start.9 = (bf16[72,128]{1,0:T(8,128)(2,1)S(1)}, bf16[72,128]{1,0:T(8,128)(2,1)S(1)}, u32[]{:S(2)}, u32[]{:S(2)}) collective-permute-start(bf16[72,128]{1,0:T(8,128)(2,1)S(1)} %slice.25), channel_id=1, source_target_pairs={{0,1},{1,0},{2,3},{3,2},{4,5},{5,4},{6,7},{7,6},{8,9},{9,8},{10,11... | collective-permute-start | bytes 55304 | tf_op jit(solution)/shard_map/ppermute | solution.py:634
  141.0 1.7 %collective-permute-done.10 = bf16[72,128]{1,0:T(8,128)(2,1)S(1)} collective-permute-done((bf16[72,128]{1,0:T(8,128)(2,1)S(1)}, bf16[72,128]{1,0:T(8,128)(2,1)S(1)}, u32[]{:S(2)}, u32[]{:S(2)}) %collective-permute-start.10) | collective-permute-done | bytes 18464 | tf_op jit(solution)/shard_map/ppermute | solution.py:634
  142.7 0.6 collective-permute-done.9
  143.3 0.0 collective-permute-done.8
  143.3 0.1 collective-permute-start.11
  143.4 1.3 collective-permute-done.11.far_ref
  144.7 0.9 unpack_gradients.1
  (5 shorter events, 0.1 us)
Async XLA Ops:
  2.3 67.0 %collective-permute-start = (bf16[576,96]{1,0:T(8,128)(2,1)}, bf16[576,96]{1,0:T(8,128)(2,1)S(1)}, u32[]{:S(2)}, u32[]{:S(2)}) collective-permute-start(bf16[576,96]{1,0:T(8,128)(2,1)} %pack_weights.1.own_ref), channel_id=1, source_target_pairs={{0,1},{1,0},{2,3},{3,2},{4,5},{5,4},{6,7},{7,6},{8,9},{9,8},{10,11... | collective-permute-start | bytes 331784 | tf_op jit(solution)/shard_map/ppermute | solution.py:634
  69.3 0.7 copy-start
  118.9 1.7 %collective-permute-start.1 = (bf16[4,192,128]{2,1,0:T(8,128)(2,1)}, bf16[4,192,128]{2,1,0:T(8,128)(2,1)S(1)}, u32[]{:S(2)}, u32[]{:S(2)}) collective-permute-start(bf16[4,192,128]{2,1,0:T(8,128)(2,1)} %get-tuple-element.33), channel_id=1, source_target_pairs={{0,2},{1,3},{2,0},{3,1},{4,6},{5,7},{6,4},{7,5},{8,10},{9,11},{10,... | collective-permute-start | bytes 589832 | tf_op jit(solution)/shard_map/ppermute | solution.py:634
  121.6 5.2 %collective-permute-start.2 = (bf16[192,128]{1,0:T(8,128)(2,1)S(1)}, bf16[192,128]{1,0:T(8,128)(2,1)S(1)}, u32[]{:S(2)}, u32[]{:S(2)}) collective-permute-start(bf16[192,128]{1,0:T(8,128)(2,1)S(1)} %get-tuple-element.44), channel_id=1, source_target_pairs={{0,1},{1,0},{2,3},{3,2},{4,5},{5,4},{6,7},{7,6},{8,9},{9,8},{10,11... | collective-permute-start | bytes 147464 | tf_op jit(solution)/shard_map/ppermute | solution.py:634
  121.7 5.1 %collective-permute-start.4 = (bf16[192,128]{1,0:T(8,128)(2,1)S(1)}, bf16[192,128]{1,0:T(8,128)(2,1)S(1)}, u32[]{:S(2)}, u32[]{:S(2)}) collective-permute-start(bf16[192,128]{1,0:T(8,128)(2,1)S(1)} %get-tuple-element.45), channel_id=1, source_target_pairs={{0,5},{1,4},{2,7},{3,6},{4,1},{5,0},{6,3},{7,2},{8,13},{9,12},{10,... | collective-permute-start | bytes 147464 | tf_op jit(solution)/shard_map/ppermute | solution.py:634
  124.7 4.1 %collective-permute-start.3 = (bf16[192,128]{1,0:T(8,128)(2,1)S(1)}, bf16[192,128]{1,0:T(8,128)(2,1)S(1)}, u32[]{:S(2)}, u32[]{:S(2)}) collective-permute-start(bf16[192,128]{1,0:T(8,128)(2,1)S(1)} %get-tuple-element.46), channel_id=1, source_target_pairs={{0,4},{1,5},{2,6},{3,7},{4,0},{5,1},{6,2},{7,3},{8,12},{9,13},{10,... | collective-permute-start | bytes 147464 | tf_op jit(solution)/shard_map/ppermute | solution.py:634
  128.8 6.1 %collective-permute-start.7 = (bf16[192,128]{1,0:T(8,128)(2,1)S(1)}, bf16[192,128]{1,0:T(8,128)(2,1)S(1)}, u32[]{:S(2)}, u32[]{:S(2)}) collective-permute-start(bf16[192,128]{1,0:T(8,128)(2,1)S(1)} %fusion.2), channel_id=1, source_target_pairs={{0,24},{1,25},{2,26},{3,27},{4,28},{5,29},{6,30},{7,31},{8,16},{9,... | collective-permute-start | bytes 147464 | tf_op jit(solution)/shard_map/ppermute | solution.py:634
  132.4 5.0 %collective-permute-start.6 = (bf16[192,128]{1,0:T(8,128)(2,1)S(1)}, bf16[192,128]{1,0:T(8,128)(2,1)S(1)}, u32[]{:S(2)}, u32[]{:S(2)}) collective-permute-start(bf16[192,128]{1,0:T(8,128)(2,1)S(1)} %fusion.2), channel_id=1, source_target_pairs={{0,16},{1,17},{2,18},{3,19},{4,20},{5,21},{6,22},{7,23},{8,24},{9,... | collective-permute-start | bytes 147464 | tf_op jit(solution)/shard_map/ppermute | solution.py:634
  132.4 5.0 %collective-permute-start.5 = (bf16[192,128]{1,0:T(8,128)(2,1)S(1)}, bf16[192,128]{1,0:T(8,128)(2,1)S(1)}, u32[]{:S(2)}, u32[]{:S(2)}) collective-permute-start(bf16[192,128]{1,0:T(8,128)(2,1)S(1)} %fusion.2), channel_id=1, source_target_pairs={{0,8},{1,9},{2,10},{3,11},{4,12},{5,13},{6,14},{7,15},{8,0},{9,1},... | collective-permute-start | bytes 147464 | tf_op jit(solution)/shard_map/ppermute | solution.py:634
  137.5 5.8 %collective-permute-start.8 = (bf16[192,128]{1,0:T(8,128)(2,1)S(1)}, bf16[192,128]{1,0:T(8,128)(2,1)S(1)}, u32[]{:S(2)}, u32[]{:S(2)}) collective-permute-start(bf16[192,128]{1,0:T(8,128)(2,1)S(1)} %add_convert_fusion.1), channel_id=1, source_target_pairs={{0,4},{1,5},{2,6},{3,7},{4,0},{5,1},{6,2},{7,3},{8,12},{9,13},{10,... | collective-permute-start | bytes 147464 | tf_op jit(solution)/shard_map/ppermute | solution.py:634
  138.1 4.7 %collective-permute-start.10 = (bf16[72,128]{1,0:T(8,128)(2,1)S(1)}, bf16[72,128]{1,0:T(8,128)(2,1)S(1)}, u32[]{:S(2)}, u32[]{:S(2)}) collective-permute-start(bf16[72,128]{1,0:T(8,128)(2,1)S(1)} %slice.25), channel_id=1, source_target_pairs={{0,5},{1,4},{2,7},{3,6},{4,1},{5,0},{6,3},{7,2},{8,13},{9,12},{10,... | collective-permute-start | bytes 55304 | tf_op jit(solution)/shard_map/ppermute | solution.py:634
  139.5 3.8 %collective-permute-start.9 = (bf16[72,128]{1,0:T(8,128)(2,1)S(1)}, bf16[72,128]{1,0:T(8,128)(2,1)S(1)}, u32[]{:S(2)}, u32[]{:S(2)}) collective-permute-start(bf16[72,128]{1,0:T(8,128)(2,1)S(1)} %slice.25), channel_id=1, source_target_pairs={{0,1},{1,0},{2,3},{3,2},{4,5},{5,4},{6,7},{7,6},{8,9},{9,8},{10,11... | collective-permute-start | bytes 55304 | tf_op jit(solution)/shard_map/ppermute | solution.py:634
  143.3 1.4 collective-permute-start.11

commit v4 on v3

--- a/solution.py
+++ b/solution.py
@@ -75,17 +75,14 @@
     before_ref,
     middle_ref,
     tap_t_ref,
-    wq_hbm,
-    wk_hbm,
-    wv_hbm,
+    wq_ref,
+    wk_ref,
+    wv_ref,
     wo_hbm,
     we_hbm,
     wr_hbm,
     top_ref,
     tap_ref,
-    wq_ref,
-    wk_ref,
-    wv_ref,
     wo_ref,
     we_ref,
     wr_ref,
@@ -96,7 +93,6 @@
     k_ref,
     v_ref,
     ctx_ref,
-    wv_t_ref,
     fine_ref,
 ):
     width = x_ref.shape[1]
@@ -108,9 +104,6 @@
         pltpu.make_async_copy(source, target, copied.at[i])
         for i, (source, target) in enumerate(
             (
-                (wq_hbm, wq_ref),
-                (wk_hbm, wk_ref),
-                (wv_hbm, wv_ref),
                 (wo_hbm, wo_ref),
                 (we_hbm, we_ref),
                 (wr_hbm, wr_ref),
@@ -120,17 +113,9 @@
 
     @pl.when(starting)
     def _():
-        for copy in copies[0:3]:
+        for copy in copies:
             copy.start()
         v_ref[:, HEAD:padded] = jnp.ones((heads, padded - HEAD, SEQ), BF16)
-
-    @pl.when(starting)
-    def _():
-        for copy in copies[0:3]:
-            copy.wait()
-        for copy in copies[3:6]:
-            copy.start()
-        wv_t_ref[...] = jnp.transpose(wv_ref[...])
 
     for part in range(2):
         rows = slice(part * SEQ // 2, (part + 1) * SEQ // 2)
@@ -142,7 +127,7 @@
         k_ref[rows] = dot(normed, wk_ref[...]).astype(BF16)
     here = lax.axis_index("side") * pl.num_programs(0) + pl.program_id(0)
     fill_mask(segment_ref[here], mask_ref)
-    v = dot(wv_t_ref[...], normed_ref[...], NT).astype(BF16)
+    v = dot(wv_ref[...], normed_ref[...], (((0,), (1,)), ((), ()))).astype(BF16)
     for head in range(heads):
         v_ref[head, 0:HEAD] = v[head * HEAD : (head + 1) * HEAD]
 
@@ -174,7 +159,7 @@
 
     @pl.when(starting)
     def _():
-        for copy in copies[3:6]:
+        for copy in copies:
             copy.wait()
 
     chunk = 1024
@@ -214,8 +199,8 @@
         in_specs=[
             whole(segment),
             pl.BlockSpec((SEQ, width), lambda i: (i, 0)),
-            *map(whole, (before, middle, tap_t)),
-            *[pl.BlockSpec(memory_space=pl.ANY)] * 6,
+            *map(whole, (before, middle, tap_t, wq, wk, wv)),
+            *[pl.BlockSpec(memory_space=pl.ANY)] * 3,
         ],
         out_specs=[
             pl.BlockSpec((SEQ, width), lambda i: (i, 0)),
@@ -226,15 +211,14 @@
             jax.ShapeDtypeStruct((side, tokens), BF16),
         ],
         scratch_shapes=[
-            *[pltpu.VMEM(w.shape, BF16) for w in (wq, wk, wv, wo, we, wr)],
-            pltpu.SemaphoreType.DMA((6,)),
+            *[pltpu.VMEM(w.shape, BF16) for w in (wo, we, wr)],
+            pltpu.SemaphoreType.DMA((3,)),
             pltpu.VMEM((SEQ, SEQ), BF16),
             pltpu.VMEM((SEQ, width), BF16),
             pltpu.VMEM((SEQ, width), BF16),
             pltpu.VMEM((SEQ, width), BF16),
             pltpu.VMEM((heads, HEAD + 16, SEQ), BF16),
             pltpu.VMEM((width, SEQ), BF16),
-            pltpu.VMEM((width, width), BF16),
             pltpu.VMEM((8, TILE), F32),
         ],
         compiler_params=pltpu.CompilerParams(vmem_limit_bytes=60 << 20),

time: 146 us -> 145 us (level)
  transfers between devices with their start and end apart: 12 -> 12, of which waited for: 8 -> 8; matrix products, arithmetic and copies ran while one was open for 0% -> 0% of each run, Pallas kernels for 44% -> 43%
where the time goes in v4:
time: 145 us; the launch traced here: 144 us
  Pallas kernels  114 us (79%)
  starting transfers between devices  14.7 us (10%)
  waiting for transfers between devices  13 us (9%)
    pallas_call x1, Pallas kernels, frozen_block(): pl.pallas_call(frozen_kernel, grid=(tokens // SEQ,), in_specs=[whole(segm...  62 us
    pallas_call x1, Pallas kernels, side_block(): pl.pallas_call(side_kernel, grid=(tokens // SEQ,), in_specs=[pl.BlockSpec...  49 us
    ppermute x12, starting transfers between devices, exchange(): return lax.ppermute(values, ('dp', 'side'), pairs)  14.7 us
    ppermute x12, waiting for transfers between devices, exchange(): return lax.ppermute(values, ('dp', 'side'), pairs)  13 us
  transfers between devices with their start and end apart: 12, of which 8 were waited for; matrix products, arithmetic and copies ran while one was open for 0% of the time, Pallas kernels for 43%

profile of v4, /device:TPU:0, one launch (start us, length us, event | category | flops | bytes accessed | tf_op | source)
XLA Modules:
  0.0 144.3 jit_solution(11716880572625221653)
XLA Ops:
  0.6 1.6 %pack_weights.1.own_ref = bf16[576,96]{1,0:T(8,128)(2,1)} custom-call(bf16[96,192]{1,0:T(8,128)(2,1)} %expand_ref.1, bf16[48,96]{1,0:T(8,128)(2,1)} %bitcast.33, bf16[48,96]{1,0:T(8,128)(2,1)} %bitcast.34, bf16[48,96]{1,0:T(8,128)(2,1)} %bitcast.35, bf16[48,96]{1,0:T(8,128)(2,1)} %output_ref.1, bf16[192,96]{1,0:T(8,128)(2,1)} %reduce_ref.1), custom_call_target="tpu_custom_call" | custom-call | tf_op jit(solution)/shard_map/pack_weights/pallas_call | solution.py:656
  2.3 3.0 %collective-permute-start = (bf16[576,96]{1,0:T(8,128)(2,1)}, bf16[576,96]{1,0:T(8,128)(2,1)S(1)}, u32[]{:S(2)}, u32[]{:S(2)}) collective-permute-start(bf16[576,96]{1,0:T(8,128)(2,1)} %pack_weights.1.own_ref), channel_id=1, source_target_pairs={{0,1},{1,0},{2,3},{3,2},{4,5},{5,4},{6,7},{7,6},{8,9},{9,8},{10,11... | collective-permute-start | bytes 331784 | tf_op jit(solution)/shard_map/ppermute | solution.py:618
  5.9 62.0 %frozen_block.1 = (bf16[2048,768]{1,0:T(8,128)(2,1)}, bf16[96,2048]{1,0:T(8,128)(2,1)}) custom-call(s32[4,1,1024]{2,1,0:T(1,128)} %bitcast.31, bf16[2048,768]{1,0:T(8,128)(2,1)} %x_ref.1, f32[768]{0:T(1024)} %before_ref.1, f32[768]{0:T(1024)} %middle_ref.1, bf16[96,768]{1,0:T(8,128)(2,1)} %bitcast.30, bf16[768,768]{1,0:T(8,128)(2,1)} %wq_ref.1, ...), custom_call_target="tpu_custom_call" | custom-call | tf_op jit(solution)/shard_map/frozen_block/pallas_call | solution.py:196
  67.9 0.0 collective-permute-done.other_ref
  68.0 0.0 copy-start
  68.0 0.6 copy-done
  68.6 49.0 %side_block.1 = (bf16[96,2048]{1,0:T(8,128)(2,1)}, bf16[96,2048]{1,0:T(8,128)(2,1)}, bf16[4,192,128]{2,1,0:T(8,128)(2,1)}, bf16[4,192,128]{2,1,0:T(8,128)(2,1)}) custom-call(s32[1]{0:T(128)S(6)} %copy.35.index_ref, s32[4,1,1024]{2,1,0:T(1,128)} %bitcast.32, bf16[96,2048]{1,0:T(8,128)(2,1)} %get-tuple-element.28.tap_ref, bf16[96,2048]{1,0:T(8,128)(2,1)} %bitcast.28, ...), custom_call_target="tpu_custom_call" | custom-call | tf_op jit(solution)/shard_map/side_block/pallas_call | solution.py:513
  117.6 0.1 collective-permute-start.1
  117.7 1.6 %collective-permute-done.1 = bf16[4,192,128]{2,1,0:T(8,128)(2,1)S(1)} collective-permute-done((bf16[4,192,128]{2,1,0:T(8,128)(2,1)}, bf16[4,192,128]{2,1,0:T(8,128)(2,1)S(1)}, u32[]{:S(2)}, u32[]{:S(2)}) %collective-permute-start.1) | collective-permute-done | bytes 196640 | tf_op jit(solution)/shard_map/ppermute | solution.py:618
  119.3 1.0 add_convert_fusion
  120.3 0.1 collective-permute-start.2
  120.4 2.9 %collective-permute-start.4 = (bf16[192,128]{1,0:T(8,128)(2,1)S(1)}, bf16[192,128]{1,0:T(8,128)(2,1)S(1)}, u32[]{:S(2)}, u32[]{:S(2)}) collective-permute-start(bf16[192,128]{1,0:T(8,128)(2,1)S(1)} %get-tuple-element.45), channel_id=1, source_target_pairs={{0,5},{1,4},{2,7},{3,6},{4,1},{5,0},{6,3},{7,2},{8,13},{9,12},{10,... | collective-permute-start | bytes 147464 | tf_op jit(solution)/shard_map/ppermute | solution.py:618
  123.3 0.5 collective-permute-start.3
  123.9 1.7 %collective-permute-done.2 = bf16[192,128]{1,0:T(8,128)(2,1)S(1)} collective-permute-done((bf16[192,128]{1,0:T(8,128)(2,1)S(1)}, bf16[192,128]{1,0:T(8,128)(2,1)S(1)}, u32[]{:S(2)}, u32[]{:S(2)}) %collective-permute-start.2) | collective-permute-done | bytes 49184 | tf_op jit(solution)/shard_map/ppermute | solution.py:618
  125.5 0.0 collective-permute-done.4
  125.5 1.9 %collective-permute-done.3 = bf16[192,128]{1,0:T(8,128)(2,1)S(1)} collective-permute-done((bf16[192,128]{1,0:T(8,128)(2,1)S(1)}, bf16[192,128]{1,0:T(8,128)(2,1)S(1)}, u32[]{:S(2)}, u32[]{:S(2)}) %collective-permute-start.3) | collective-permute-done | bytes 49184 | tf_op jit(solution)/shard_map/ppermute | solution.py:618
  127.4 3.7 %collective-permute-start.7 = (bf16[192,128]{1,0:T(8,128)(2,1)S(1)}, bf16[192,128]{1,0:T(8,128)(2,1)S(1)}, u32[]{:S(2)}, u32[]{:S(2)}) collective-permute-start(bf16[192,128]{1,0:T(8,128)(2,1)S(1)} %fusion.2), channel_id=1, source_target_pairs={{0,24},{1,25},{2,26},{3,27},{4,28},{5,29},{6,30},{7,31},{8,16},{9,... | collective-permute-start | bytes 147464 | tf_op jit(solution)/shard_map/ppermute | solution.py:618
  131.1 0.0 collective-permute-start.6
  131.1 0.8 collective-permute-start.5
  131.9 1.6 %collective-permute-done.7 = bf16[192,128]{1,0:T(8,128)(2,1)S(1)} collective-permute-done((bf16[192,128]{1,0:T(8,128)(2,1)S(1)}, bf16[192,128]{1,0:T(8,128)(2,1)S(1)}, u32[]{:S(2)}, u32[]{:S(2)}) %collective-permute-start.7) | collective-permute-done | bytes 49184 | tf_op jit(solution)/shard_map/ppermute | solution.py:618
  133.5 2.6 %collective-permute-done.6 = bf16[192,128]{1,0:T(8,128)(2,1)S(1)} collective-permute-done((bf16[192,128]{1,0:T(8,128)(2,1)S(1)}, bf16[192,128]{1,0:T(8,128)(2,1)S(1)}, u32[]{:S(2)}, u32[]{:S(2)}) %collective-permute-start.6) | collective-permute-done | bytes 49184 | tf_op jit(solution)/shard_map/ppermute | solution.py:618
  136.1 0.0 collective-permute-done.5
  136.2 0.6 collective-permute-start.8
  136.7 1.5 %collective-permute-start.10 = (bf16[72,128]{1,0:T(8,128)(2,1)S(1)}, bf16[72,128]{1,0:T(8,128)(2,1)S(1)}, u32[]{:S(2)}, u32[]{:S(2)}) collective-permute-start(bf16[72,128]{1,0:T(8,128)(2,1)S(1)} %slice.25), channel_id=1, source_target_pairs={{0,5},{1,4},{2,7},{3,6},{4,1},{5,0},{6,3},{7,2},{8,13},{9,12},{10,... | collective-permute-start | bytes 55304 | tf_op jit(solution)/shard_map/ppermute | solution.py:618
  138.2 1.5 %collective-permute-start.9 = (bf16[72,128]{1,0:T(8,128)(2,1)S(1)}, bf16[72,128]{1,0:T(8,128)(2,1)S(1)}, u32[]{:S(2)}, u32[]{:S(2)}) collective-permute-start(bf16[72,128]{1,0:T(8,128)(2,1)S(1)} %slice.25), channel_id=1, source_target_pairs={{0,1},{1,0},{2,3},{3,2},{4,5},{5,4},{6,7},{7,6},{8,9},{9,8},{10,11... | collective-permute-start | bytes 55304 | tf_op jit(solution)/shard_map/ppermute | solution.py:618
  139.7 1.7 %collective-permute-done.10 = bf16[72,128]{1,0:T(8,128)(2,1)S(1)} collective-permute-done((bf16[72,128]{1,0:T(8,128)(2,1)S(1)}, bf16[72,128]{1,0:T(8,128)(2,1)S(1)}, u32[]{:S(2)}, u32[]{:S(2)}) %collective-permute-start.10) | collective-permute-done | bytes 18464 | tf_op jit(solution)/shard_map/ppermute | solution.py:618
  141.4 0.6 collective-permute-done.9
  142.0 0.0 collective-permute-done.8
  142.0 0.1 collective-permute-start.11
  142.1 1.3 collective-permute-done.11.far_ref
  143.4 0.9 unpack_gradients.1
  (5 shorter events, 0.1 us)
Async XLA Ops:
  2.3 65.7 %collective-permute-start = (bf16[576,96]{1,0:T(8,128)(2,1)}, bf16[576,96]{1,0:T(8,128)(2,1)S(1)}, u32[]{:S(2)}, u32[]{:S(2)}) collective-permute-start(bf16[576,96]{1,0:T(8,128)(2,1)} %pack_weights.1.own_ref), channel_id=1, source_target_pairs={{0,1},{1,0},{2,3},{3,2},{4,5},{5,4},{6,7},{7,6},{8,9},{9,8},{10,11... | collective-permute-start | bytes 331784 | tf_op jit(solution)/shard_map/ppermute | solution.py:618
  68.0 0.7 copy-start
  117.6 1.7 %collective-permute-start.1 = (bf16[4,192,128]{2,1,0:T(8,128)(2,1)}, bf16[4,192,128]{2,1,0:T(8,128)(2,1)S(1)}, u32[]{:S(2)}, u32[]{:S(2)}) collective-permute-start(bf16[4,192,128]{2,1,0:T(8,128)(2,1)} %get-tuple-element.33), channel_id=1, source_target_pairs={{0,2},{1,3},{2,0},{3,1},{4,6},{5,7},{6,4},{7,5},{8,10},{9,11},{10,... | collective-permute-start | bytes 589832 | tf_op jit(solution)/shard_map/ppermute | solution.py:618
  120.3 5.2 %collective-permute-start.2 = (bf16[192,128]{1,0:T(8,128)(2,1)S(1)}, bf16[192,128]{1,0:T(8,128)(2,1)S(1)}, u32[]{:S(2)}, u32[]{:S(2)}) collective-permute-start(bf16[192,128]{1,0:T(8,128)(2,1)S(1)} %get-tuple-element.44), channel_id=1, source_target_pairs={{0,1},{1,0},{2,3},{3,2},{4,5},{5,4},{6,7},{7,6},{8,9},{9,8},{10,11... | collective-permute-start | bytes 147464 | tf_op jit(solution)/shard_map/ppermute | solution.py:618
  120.4 5.1 %collective-permute-start.4 = (bf16[192,128]{1,0:T(8,128)(2,1)S(1)}, bf16[192,128]{1,0:T(8,128)(2,1)S(1)}, u32[]{:S(2)}, u32[]{:S(2)}) collective-permute-start(bf16[192,128]{1,0:T(8,128)(2,1)S(1)} %get-tuple-element.45), channel_id=1, source_target_pairs={{0,5},{1,4},{2,7},{3,6},{4,1},{5,0},{6,3},{7,2},{8,13},{9,12},{10,... | collective-permute-start | bytes 147464 | tf_op jit(solution)/shard_map/ppermute | solution.py:618
  123.3 4.1 %collective-permute-start.3 = (bf16[192,128]{1,0:T(8,128)(2,1)S(1)}, bf16[192,128]{1,0:T(8,128)(2,1)S(1)}, u32[]{:S(2)}, u32[]{:S(2)}) collective-permute-start(bf16[192,128]{1,0:T(8,128)(2,1)S(1)} %get-tuple-element.46), channel_id=1, source_target_pairs={{0,4},{1,5},{2,6},{3,7},{4,0},{5,1},{6,2},{7,3},{8,12},{9,13},{10,... | collective-permute-start | bytes 147464 | tf_op jit(solution)/shard_map/ppermute | solution.py:618
  127.4 6.1 %collective-permute-start.7 = (bf16[192,128]{1,0:T(8,128)(2,1)S(1)}, bf16[192,128]{1,0:T(8,128)(2,1)S(1)}, u32[]{:S(2)}, u32[]{:S(2)}) collective-permute-start(bf16[192,128]{1,0:T(8,128)(2,1)S(1)} %fusion.2), channel_id=1, source_target_pairs={{0,24},{1,25},{2,26},{3,27},{4,28},{5,29},{6,30},{7,31},{8,16},{9,... | collective-permute-start | bytes 147464 | tf_op jit(solution)/shard_map/ppermute | solution.py:618
  131.1 5.0 %collective-permute-start.6 = (bf16[192,128]{1,0:T(8,128)(2,1)S(1)}, bf16[192,128]{1,0:T(8,128)(2,1)S(1)}, u32[]{:S(2)}, u32[]{:S(2)}) collective-permute-start(bf16[192,128]{1,0:T(8,128)(2,1)S(1)} %fusion.2), channel_id=1, source_target_pairs={{0,16},{1,17},{2,18},{3,19},{4,20},{5,21},{6,22},{7,23},{8,24},{9,... | collective-permute-start | bytes 147464 | tf_op jit(solution)/shard_map/ppermute | solution.py:618
  131.1 5.0 %collective-permute-start.5 = (bf16[192,128]{1,0:T(8,128)(2,1)S(1)}, bf16[192,128]{1,0:T(8,128)(2,1)S(1)}, u32[]{:S(2)}, u32[]{:S(2)}) collective-permute-start(bf16[192,128]{1,0:T(8,128)(2,1)S(1)} %fusion.2), channel_id=1, source_target_pairs={{0,8},{1,9},{2,10},{3,11},{4,12},{5,13},{6,14},{7,15},{8,0},{9,1},... | collective-permute-start | bytes 147464 | tf_op jit(solution)/shard_map/ppermute | solution.py:618
  136.2 5.8 %collective-permute-start.8 = (bf16[192,128]{1,0:T(8,128)(2,1)S(1)}, bf16[192,128]{1,0:T(8,128)(2,1)S(1)}, u32[]{:S(2)}, u32[]{:S(2)}) collective-permute-start(bf16[192,128]{1,0:T(8,128)(2,1)S(1)} %add_convert_fusion.1), channel_id=1, source_target_pairs={{0,4},{1,5},{2,6},{3,7},{4,0},{5,1},{6,2},{7,3},{8,12},{9,13},{10,... | collective-permute-start | bytes 147464 | tf_op jit(solution)/shard_map/ppermute | solution.py:618
  136.7 4.7 %collective-permute-start.10 = (bf16[72,128]{1,0:T(8,128)(2,1)S(1)}, bf16[72,128]{1,0:T(8,128)(2,1)S(1)}, u32[]{:S(2)}, u32[]{:S(2)}) collective-permute-start(bf16[72,128]{1,0:T(8,128)(2,1)S(1)} %slice.25), channel_id=1, source_target_pairs={{0,5},{1,4},{2,7},{3,6},{4,1},{5,0},{6,3},{7,2},{8,13},{9,12},{10,... | collective-permute-start | bytes 55304 | tf_op jit(solution)/shard_map/ppermute | solution.py:618
  138.2 3.8 %collective-permute-start.9 = (bf16[72,128]{1,0:T(8,128)(2,1)S(1)}, bf16[72,128]{1,0:T(8,128)(2,1)S(1)}, u32[]{:S(2)}, u32[]{:S(2)}) collective-permute-start(bf16[72,128]{1,0:T(8,128)(2,1)S(1)} %slice.25), channel_id=1, source_target_pairs={{0,1},{1,0},{2,3},{3,2},{4,5},{5,4},{6,7},{7,6},{8,9},{9,8},{10,11... | collective-permute-start | bytes 55304 | tf_op jit(solution)/shard_map/ppermute | solution.py:618
  142.0 1.4 collective-permute-start.11

commit v5 on v4

--- a/solution.py
+++ b/solution.py
@@ -246,7 +246,7 @@
     tap_ref,
     stream_ref,
     up_ref,
-    top_ref,
+    top_hbm,
     table_ref,
     before_ref,
     middle_ref,
@@ -278,6 +278,8 @@
     dctx_ref,
     dqkv_ref,
     fine_ref,
+    top_ref,
+    copied,
 ):
     side = tap_ref.shape[0]
     heads = side // SIDE_HEAD
@@ -380,6 +382,9 @@
 
         lax.fori_loop(0, heads // together, step, 0)
 
+    lines = pl.ds(pl.multiple_of(pl.program_id(0) * SEQ, SEQ), SEQ)
+    top_copy = pltpu.make_async_copy(top_hbm.at[lines], top_ref, copied)
+    top_copy.start()
     fine_ref[...] = jnp.ones_like(fine_ref)
     attend(False, TILE)
     pl.when(jnp.min(fine_ref[...]) < 0.5)(lambda: attend(True, TILE))
@@ -448,6 +453,7 @@
 
     lax.fori_loop(0, heads // GROUP, back_group, 0)
 
+    top_copy.wait()
     dqkv = dqkv_ref[...].astype(BF16)
     qkv_grad_ref[...] += dot(n1, dqkv, NT)
     dn1 = dot(w_ref[...], dqkv, TN)
@@ -519,7 +525,7 @@
             lanes(side),
             lanes(side),
             lanes(side),
-            pl.BlockSpec((SEQ, width), lambda i: (i, 0)),
+            pl.BlockSpec(memory_space=pl.ANY),
             *map(whole, (table, before, middle, own, other)),
         ],
         out_specs=[lanes(side), lanes(side), packed, packed],
@@ -552,6 +558,8 @@
             pltpu.VMEM((side, SEQ), F32),
             pltpu.VMEM((3 * side, SEQ), F32),
             pltpu.VMEM((8, TILE), F32),
+            pltpu.VMEM((SEQ, width), BF16),
+            pltpu.SemaphoreType.DMA,
         ],
         compiler_params=pltpu.CompilerParams(vmem_limit_bytes=60 << 20),
         name="side_block",

time: 145 us -> 144 us (level)
  no operation moved by 1% of the time
where the time goes in v5:
time: 144 us
  Pallas kernels  113 us (78%)
  starting transfers between devices  14.7 us (10%)
  waiting for transfers between devices  13.1 us (9%)
    pallas_call x1, Pallas kernels, frozen_block(): pl.pallas_call(frozen_kernel, grid=(tokens // SEQ,), in_specs=[whole(segm...  62 us
    pallas_call x1, Pallas kernels, side_block(): pl.pallas_call(side_kernel, grid=(tokens // SEQ,), in_specs=[pl.BlockSpec...  48.5 us
    ppermute x12, starting transfers between devices, exchange(): return lax.ppermute(values, ('dp', 'side'), pairs)  14.7 us
    ppermute x12, waiting for transfers between devices, exchange(): return lax.ppermute(values, ('dp', 'side'), pairs)  13.1 us
  transfers between devices with their start and end apart: 12, of which 8 were waited for; matrix products, arithmetic and copies ran while one was open for 0% of the time, Pallas kernels for 43%

profile of v5, /device:TPU:0, one launch (start us, length us, event | category | flops | bytes accessed | tf_op | source)
XLA Modules:
  0.0 143.9 jit_solution(4214698228800025989)
XLA Ops:
  0.6 1.6 %pack_weights.1.own_ref = bf16[576,96]{1,0:T(8,128)(2,1)} custom-call(bf16[96,192]{1,0:T(8,128)(2,1)} %expand_ref.1, bf16[48,96]{1,0:T(8,128)(2,1)} %bitcast.33, bf16[48,96]{1,0:T(8,128)(2,1)} %bitcast.34, bf16[48,96]{1,0:T(8,128)(2,1)} %bitcast.35, bf16[48,96]{1,0:T(8,128)(2,1)} %output_ref.1, bf16[192,96]{1,0:T(8,128)(2,1)} %reduce_ref.1), custom_call_target="tpu_custom_call" | custom-call | tf_op jit(solution)/shard_map/pack_weights/pallas_call | solution.py:664
  2.3 3.0 %collective-permute-start = (bf16[576,96]{1,0:T(8,128)(2,1)}, bf16[576,96]{1,0:T(8,128)(2,1)S(1)}, u32[]{:S(2)}, u32[]{:S(2)}) collective-permute-start(bf16[576,96]{1,0:T(8,128)(2,1)} %pack_weights.1.own_ref), channel_id=1, source_target_pairs={{0,1},{1,0},{2,3},{3,2},{4,5},{5,4},{6,7},{7,6},{8,9},{9,8},{10,11... | collective-permute-start | bytes 331784 | tf_op jit(solution)/shard_map/ppermute | solution.py:626
  5.9 62.0 %frozen_block.1 = (bf16[2048,768]{1,0:T(8,128)(2,1)}, bf16[96,2048]{1,0:T(8,128)(2,1)}) custom-call(s32[4,1,1024]{2,1,0:T(1,128)} %bitcast.31, bf16[2048,768]{1,0:T(8,128)(2,1)} %x_ref.1, f32[768]{0:T(1024)} %before_ref.1, f32[768]{0:T(1024)} %middle_ref.1, bf16[96,768]{1,0:T(8,128)(2,1)} %bitcast.30, bf16[768,768]{1,0:T(8,128)(2,1)} %wq_ref.1, ...), custom_call_target="tpu_custom_call" | custom-call | tf_op jit(solution)/shard_map/frozen_block/pallas_call | solution.py:196
  67.9 0.0 collective-permute-done.other_ref
  68.0 0.0 copy-start
  68.0 0.6 copy-done
  68.6 48.5 %side_block.1 = (bf16[96,2048]{1,0:T(8,128)(2,1)}, bf16[96,2048]{1,0:T(8,128)(2,1)}, bf16[4,192,128]{2,1,0:T(8,128)(2,1)}, bf16[4,192,128]{2,1,0:T(8,128)(2,1)}) custom-call(s32[1]{0:T(128)S(6)} %copy.35.index_ref, s32[4,1,1024]{2,1,0:T(1,128)} %bitcast.32, bf16[96,2048]{1,0:T(8,128)(2,1)} %get-tuple-element.28.tap_ref, bf16[96,2048]{1,0:T(8,128)(2,1)} %bitcast.28, ...), custom_call_target="tpu_custom_call" | custom-call | tf_op jit(solution)/shard_map/side_block/pallas_call | solution.py:519
  117.1 0.1 collective-permute-start.1
  117.2 1.6 %collective-permute-done.1 = bf16[4,192,128]{2,1,0:T(8,128)(2,1)S(1)} collective-permute-done((bf16[4,192,128]{2,1,0:T(8,128)(2,1)}, bf16[4,192,128]{2,1,0:T(8,128)(2,1)S(1)}, u32[]{:S(2)}, u32[]{:S(2)}) %collective-permute-start.1) | collective-permute-done | bytes 196640 | tf_op jit(solution)/shard_map/ppermute | solution.py:626
  118.8 1.0 add_convert_fusion
  119.8 0.1 collective-permute-start.2
  120.0 2.9 %collective-permute-start.4 = (bf16[192,128]{1,0:T(8,128)(2,1)S(1)}, bf16[192,128]{1,0:T(8,128)(2,1)S(1)}, u32[]{:S(2)}, u32[]{:S(2)}) collective-permute-start(bf16[192,128]{1,0:T(8,128)(2,1)S(1)} %get-tuple-element.45), channel_id=1, source_target_pairs={{0,5},{1,4},{2,7},{3,6},{4,1},{5,0},{6,3},{7,2},{8,13},{9,12},{10,... | collective-permute-start | bytes 147464 | tf_op jit(solution)/shard_map/ppermute | solution.py:626
  122.9 0.5 collective-permute-start.3
  123.4 1.7 %collective-permute-done.2 = bf16[192,128]{1,0:T(8,128)(2,1)S(1)} collective-permute-done((bf16[192,128]{1,0:T(8,128)(2,1)S(1)}, bf16[192,128]{1,0:T(8,128)(2,1)S(1)}, u32[]{:S(2)}, u32[]{:S(2)}) %collective-permute-start.2) | collective-permute-done | bytes 49184 | tf_op jit(solution)/shard_map/ppermute | solution.py:626
  125.0 0.0 collective-permute-done.4
  125.0 1.9 %collective-permute-done.3 = bf16[192,128]{1,0:T(8,128)(2,1)S(1)} collective-permute-done((bf16[192,128]{1,0:T(8,128)(2,1)S(1)}, bf16[192,128]{1,0:T(8,128)(2,1)S(1)}, u32[]{:S(2)}, u32[]{:S(2)}) %collective-permute-start.3) | collective-permute-done | bytes 49184 | tf_op jit(solution)/shard_map/ppermute | solution.py:626
  127.0 3.7 %collective-permute-start.7 = (bf16[192,128]{1,0:T(8,128)(2,1)S(1)}, bf16[192,128]{1,0:T(8,128)(2,1)S(1)}, u32[]{:S(2)}, u32[]{:S(2)}) collective-permute-start(bf16[192,128]{1,0:T(8,128)(2,1)S(1)} %fusion.2), channel_id=1, source_target_pairs={{0,24},{1,25},{2,26},{3,27},{4,28},{5,29},{6,30},{7,31},{8,16},{9,... | collective-permute-start | bytes 147464 | tf_op jit(solution)/shard_map/ppermute | solution.py:626
  130.6 0.0 collective-permute-start.6
  130.7 0.8 collective-permute-start.5
  131.4 1.7 %collective-permute-done.7 = bf16[192,128]{1,0:T(8,128)(2,1)S(1)} collective-permute-done((bf16[192,128]{1,0:T(8,128)(2,1)S(1)}, bf16[192,128]{1,0:T(8,128)(2,1)S(1)}, u32[]{:S(2)}, u32[]{:S(2)}) %collective-permute-start.7) | collective-permute-done | bytes 49184 | tf_op jit(solution)/shard_map/ppermute | solution.py:626
  133.1 2.6 %collective-permute-done.6 = bf16[192,128]{1,0:T(8,128)(2,1)S(1)} collective-permute-done((bf16[192,128]{1,0:T(8,128)(2,1)S(1)}, bf16[192,128]{1,0:T(8,128)(2,1)S(1)}, u32[]{:S(2)}, u32[]{:S(2)}) %collective-permute-start.6) | collective-permute-done | bytes 49184 | tf_op jit(solution)/shard_map/ppermute | solution.py:626
  135.6 0.0 collective-permute-done.5
  135.7 0.6 collective-permute-start.8
  136.3 1.5 %collective-permute-start.10 = (bf16[72,128]{1,0:T(8,128)(2,1)S(1)}, bf16[72,128]{1,0:T(8,128)(2,1)S(1)}, u32[]{:S(2)}, u32[]{:S(2)}) collective-permute-start(bf16[72,128]{1,0:T(8,128)(2,1)S(1)} %slice.25), channel_id=1, source_target_pairs={{0,5},{1,4},{2,7},{3,6},{4,1},{5,0},{6,3},{7,2},{8,13},{9,12},{10,... | collective-permute-start | bytes 55304 | tf_op jit(solution)/shard_map/ppermute | solution.py:626
  137.8 1.5 %collective-permute-start.9 = (bf16[72,128]{1,0:T(8,128)(2,1)S(1)}, bf16[72,128]{1,0:T(8,128)(2,1)S(1)}, u32[]{:S(2)}, u32[]{:S(2)}) collective-permute-start(bf16[72,128]{1,0:T(8,128)(2,1)S(1)} %slice.25), channel_id=1, source_target_pairs={{0,1},{1,0},{2,3},{3,2},{4,5},{5,4},{6,7},{7,6},{8,9},{9,8},{10,11... | collective-permute-start | bytes 55304 | tf_op jit(solution)/shard_map/ppermute | solution.py:626
  139.2 1.7 %collective-permute-done.10 = bf16[72,128]{1,0:T(8,128)(2,1)S(1)} collective-permute-done((bf16[72,128]{1,0:T(8,128)(2,1)S(1)}, bf16[72,128]{1,0:T(8,128)(2,1)S(1)}, u32[]{:S(2)}, u32[]{:S(2)}) %collective-permute-start.10) | collective-permute-done | bytes 18464 | tf_op jit(solution)/shard_map/ppermute | solution.py:626
  140.9 0.6 collective-permute-done.9
  141.5 0.0 collective-permute-done.8
  141.6 0.1 collective-permute-start.11
  141.6 1.3 collective-permute-done.11.far_ref
  143.0 0.9 unpack_gradients.1
  (5 shorter events, 0.1 us)
Async XLA Ops:
  2.3 65.7 %collective-permute-start = (bf16[576,96]{1,0:T(8,128)(2,1)}, bf16[576,96]{1,0:T(8,128)(2,1)S(1)}, u32[]{:S(2)}, u32[]{:S(2)}) collective-permute-start(bf16[576,96]{1,0:T(8,128)(2,1)} %pack_weights.1.own_ref), channel_id=1, source_target_pairs={{0,1},{1,0},{2,3},{3,2},{4,5},{5,4},{6,7},{7,6},{8,9},{9,8},{10,11... | collective-permute-start | bytes 331784 | tf_op jit(solution)/shard_map/ppermute | solution.py:626
  68.0 0.7 copy-start
  117.1 1.7 %collective-permute-start.1 = (bf16[4,192,128]{2,1,0:T(8,128)(2,1)}, bf16[4,192,128]{2,1,0:T(8,128)(2,1)S(1)}, u32[]{:S(2)}, u32[]{:S(2)}) collective-permute-start(bf16[4,192,128]{2,1,0:T(8,128)(2,1)} %get-tuple-element.33), channel_id=1, source_target_pairs={{0,2},{1,3},{2,0},{3,1},{4,6},{5,7},{6,4},{7,5},{8,10},{9,11},{10,... | collective-permute-start | bytes 589832 | tf_op jit(solution)/shard_map/ppermute | solution.py:626
  119.8 5.2 %collective-permute-start.2 = (bf16[192,128]{1,0:T(8,128)(2,1)S(1)}, bf16[192,128]{1,0:T(8,128)(2,1)S(1)}, u32[]{:S(2)}, u32[]{:S(2)}) collective-permute-start(bf16[192,128]{1,0:T(8,128)(2,1)S(1)} %get-tuple-element.44), channel_id=1, source_target_pairs={{0,1},{1,0},{2,3},{3,2},{4,5},{5,4},{6,7},{7,6},{8,9},{9,8},{10,11... | collective-permute-start | bytes 147464 | tf_op jit(solution)/shard_map/ppermute | solution.py:626
  120.0 5.1 %collective-permute-start.4 = (bf16[192,128]{1,0:T(8,128)(2,1)S(1)}, bf16[192,128]{1,0:T(8,128)(2,1)S(1)}, u32[]{:S(2)}, u32[]{:S(2)}) collective-permute-start(bf16[192,128]{1,0:T(8,128)(2,1)S(1)} %get-tuple-element.45), channel_id=1, source_target_pairs={{0,5},{1,4},{2,7},{3,6},{4,1},{5,0},{6,3},{7,2},{8,13},{9,12},{10,... | collective-permute-start | bytes 147464 | tf_op jit(solution)/shard_map/ppermute | solution.py:626
  122.9 4.1 %collective-permute-start.3 = (bf16[192,128]{1,0:T(8,128)(2,1)S(1)}, bf16[192,128]{1,0:T(8,128)(2,1)S(1)}, u32[]{:S(2)}, u32[]{:S(2)}) collective-permute-start(bf16[192,128]{1,0:T(8,128)(2,1)S(1)} %get-tuple-element.46), channel_id=1, source_target_pairs={{0,4},{1,5},{2,6},{3,7},{4,0},{5,1},{6,2},{7,3},{8,12},{9,13},{10,... | collective-permute-start | bytes 147464 | tf_op jit(solution)/shard_map/ppermute | solution.py:626
  127.0 6.1 %collective-permute-start.7 = (bf16[192,128]{1,0:T(8,128)(2,1)S(1)}, bf16[192,128]{1,0:T(8,128)(2,1)S(1)}, u32[]{:S(2)}, u32[]{:S(2)}) collective-permute-start(bf16[192,128]{1,0:T(8,128)(2,1)S(1)} %fusion.2), channel_id=1, source_target_pairs={{0,24},{1,25},{2,26},{3,27},{4,28},{5,29},{6,30},{7,31},{8,16},{9,... | collective-permute-start | bytes 147464 | tf_op jit(solution)/shard_map/ppermute | solution.py:626
  130.6 5.0 %collective-permute-start.6 = (bf16[192,128]{1,0:T(8,128)(2,1)S(1)}, bf16[192,128]{1,0:T(8,128)(2,1)S(1)}, u32[]{:S(2)}, u32[]{:S(2)}) collective-permute-start(bf16[192,128]{1,0:T(8,128)(2,1)S(1)} %fusion.2), channel_id=1, source_target_pairs={{0,16},{1,17},{2,18},{3,19},{4,20},{5,21},{6,22},{7,23},{8,24},{9,... | collective-permute-start | bytes 147464 | tf_op jit(solution)/shard_map/ppermute | solution.py:626
  130.7 5.0 %collective-permute-start.5 = (bf16[192,128]{1,0:T(8,128)(2,1)S(1)}, bf16[192,128]{1,0:T(8,128)(2,1)S(1)}, u32[]{:S(2)}, u32[]{:S(2)}) collective-permute-start(bf16[192,128]{1,0:T(8,128)(2,1)S(1)} %fusion.2), channel_id=1, source_target_pairs={{0,8},{1,9},{2,10},{3,11},{4,12},{5,13},{6,14},{7,15},{8,0},{9,1},... | collective-permute-start | bytes 147464 | tf_op jit(solution)/shard_map/ppermute | solution.py:626
  135.7 5.9 %collective-permute-start.8 = (bf16[192,128]{1,0:T(8,128)(2,1)S(1)}, bf16[192,128]{1,0:T(8,128)(2,1)S(1)}, u32[]{:S(2)}, u32[]{:S(2)}) collective-permute-start(bf16[192,128]{1,0:T(8,128)(2,1)S(1)} %add_convert_fusion.1), channel_id=1, source_target_pairs={{0,4},{1,5},{2,6},{3,7},{4,0},{5,1},{6,2},{7,3},{8,12},{9,13},{10,... | collective-permute-start | bytes 147464 | tf_op jit(solution)/shard_map/ppermute | solution.py:626
  136.3 4.7 %collective-permute-start.10 = (bf16[72,128]{1,0:T(8,128)(2,1)S(1)}, bf16[72,128]{1,0:T(8,128)(2,1)S(1)}, u32[]{:S(2)}, u32[]{:S(2)}) collective-permute-start(bf16[72,128]{1,0:T(8,128)(2,1)S(1)} %slice.25), channel_id=1, source_target_pairs={{0,5},{1,4},{2,7},{3,6},{4,1},{5,0},{6,3},{7,2},{8,13},{9,12},{10,... | collective-permute-start | bytes 55304 | tf_op jit(solution)/shard_map/ppermute | solution.py:626
  137.8 3.8 %collective-permute-start.9 = (bf16[72,128]{1,0:T(8,128)(2,1)S(1)}, bf16[72,128]{1,0:T(8,128)(2,1)S(1)}, u32[]{:S(2)}, u32[]{:S(2)}) collective-permute-start(bf16[72,128]{1,0:T(8,128)(2,1)S(1)} %slice.25), channel_id=1, source_target_pairs={{0,1},{1,0},{2,3},{3,2},{4,5},{5,4},{6,7},{7,6},{8,9},{9,8},{10,11... | collective-permute-start | bytes 55304 | tf_op jit(solution)/shard_map/ppermute | solution.py:626
  141.6 1.4 collective-permute-start.11
